TPU v7x, 32 devices: a whole 2x2x4 slice. The times are simulated.
32 devices in a mesh: groups: 2 (over x), river: 8 (over z, y), hand: 2 (over core).
Axes of the slice: x: 2, y: 2, z: 4, core: 2. Of those that a mesh axis runs over, the one named last changes fastest.
Arguments:
- hand_rank: int32 [192, 1326], P(('groups', 'river'), 'hand'), parts along dimension 0, may hold values from -1 to 7461, as said below
- loads: int32 [16], P('groups'), parts along dimension 0, may hold values from 3 to 12, as said below
- turn_cards: int32 [8], P('groups'), parts along dimension 0, may hold values from 0 to 51, as said below
- turn_children: int32 [6, 16], replicated, may hold values from 0 to 1, as said below
- turn_parents: int32 [6, 16], replicated, may hold values from 0 to 1, as said below
- river_children: int32 [16, 64], replicated, may hold values from 0 to 1, as said below
- river_parents: int32 [16, 80], replicated, may hold values from 0 to 1, as said below
- showdown_pot: float32 [64, 64], replicated, may hold values from 0 to 0.0625
- river_fold: float32 [64, 64], replicated, may hold values from -0.75 to 0.75
- turn_fold: float32 [16, 16], replicated, may hold values from -1.5 to 1.5
- mover_turn: float32 [32, 1326], P('groups', 'hand'), parts along dimension 0, may hold values from 0 to 2
- mover_river: float32 [192, 64, 1326], P(('groups', 'river'), None, 'hand'), parts along dimension 0, may hold values from 0 to 120
- mover_turn_price: float32 [12, 1326], P('groups', 'hand'), parts along dimension 0, may hold values from -6 to 6
- mover_river_price: float32 [192, 16, 1326], P(('groups', 'river'), None, 'hand'), parts along dimension 0, may hold values from -120 to 120
- rival_turn: float32 [32, 1326], P('groups', 'hand'), parts along dimension 0, may hold values from 0 to 2
- rival_river: float32 [192, 64, 1326], P(('groups', 'river'), None, 'hand'), parts along dimension 0, may hold values from 0 to 120
- rival_turn_price: float32 [12, 1326], P('groups', 'hand'), parts along dimension 0, may hold values from -6 to 6
- rival_river_price: float32 [192, 16, 1326], P(('groups', 'river'), None, 'hand'), parts along dimension 0, may hold values from -120 to 120
Outputs:
- next_mover_turn: float32 [32, 1326], P('groups', 'hand'), parts along dimension 0
- next_mover_river: float32 [192, 64, 1326], P(('groups', 'river'), None, 'hand'), parts along dimension 0
- next_mover_turn_price: float32 [12, 1326], P('groups', 'hand'), parts along dimension 0
- next_mover_river_price: float32 [192, 16, 1326], P(('groups', 'river'), None, 'hand'), parts along dimension 0
- next_rival_turn: float32 [32, 1326], P('groups', 'hand'), parts along dimension 0
- next_rival_river: float32 [192, 64, 1326], P(('groups', 'river'), None, 'hand'), parts along dimension 0
- next_rival_turn_price: float32 [12, 1326], P('groups', 'hand'), parts along dimension 0
- next_rival_river_price: float32 [192, 16, 1326], P(('groups', 'river'), None, 'hand'), parts along dimension 0
There are 2 independent parts, one for each index of `groups`. A program takes and returns all parts, laid end to end along the dimension named above; an argument that names none is the same for every part. Nothing has to cross between parts.
Inputs may be any that keep to these rules, and one draw needn't show every extreme that they name: hand_rank is -1 exactly where a hand holds one of turn_cards or the slot's river card, and on every hand of an unused slot; the used slots of the river devices, taken in order, hold the 48 cards not in turn_cards, once each. The loads sum to 48; some river device holds 12. `turn_cards`: four different cards. `turn_children`: each turn sequence starts at exactly one decision point; each decision point starts one or more sequences, in a run of consecutive indices, the runs in order of the decision points. `turn_parents`: decision point 0 has no parent sequence; every other one has exactly one, a sequence starting at an earlier decision point. `river_children`: each river sequence starts at exactly one decision point; each decision point starts one or more sequences, in a run of consecutive indices, the runs in order of the decision points. `river_parents`: every river decision point has exactly one parent: a river sequence starting at an earlier decision point, or a turn sequence (the last 16 columns); decision point 0 has a turn sequence.
All inputs are finite; a program needn't handle non-finite values.
Results may differ from a plain program's by a relative error of at most 0.0003.
Values sent between devices are 32-bit elements; how exact they have to be, the bound alone decides.
No kernel may reach another device: no remote copies, remote signals or barrier semaphores. Data moves between devices by JAX's collectives and lax.ppermute only.
A program may use at most 192 MiB of HBM per device.

v0:
```python
import jax
import jax.numpy as jnp
import numpy as np
from jax import lax
from jax.sharding import PartitionSpec as P

CARDS = 52
H = 1326
ITERS = 2


HIGH = lax.Precision.HIGHEST
STEP_SCALE = 0.25
EPSILON = 1e-06


def card_tables():
    pairs = np.triu_indices(CARDS, 1)
    return (jnp.asarray(pairs[0].astype(np.int32)), jnp.asarray(pairs[1].astype(np.int32)))


def turn_alive(card_one, card_two, turn_cards):
    held = (
        (card_one[:, None] == turn_cards[None, :]) | (card_two[:, None] == turn_cards[None, :])
    ).any(axis=1)
    return 1.0 - held.astype(jnp.float32)


def pair_blocks(
    rank_near, live_near, one_near, two_near, rank_far, live_far, one_far, two_far, direction
):
    shared = (
        (one_near[:, None] == one_far[None, :])
        | (one_near[:, None] == two_far[None, :])
        | (two_near[:, None] == one_far[None, :])
        | (two_near[:, None] == two_far[None, :])
    )
    indicator = (1.0 - shared.astype(jnp.float32)) * live_near[:, None] * live_far[None, :]
    signs = jnp.sign(rank_far[None, :] - rank_near[:, None]).astype(jnp.float32) * direction
    return jnp.stack([signs * indicator, indicator])


def group_size(boards, most):
    best = 1
    for count in range(1, most + 1):
        if boards % count == 0:
            best = count
    return best


def grouped(array, count):
    return array.reshape((array.shape[0] // count, count) + array.shape[1:])


def local(
    hand_rank,
    loads,
    turn_cards,
    turn_children,
    turn_parents,
    river_children,
    river_parents,
    showdown_pot,
    river_fold,
    turn_fold,
    mover_turn,
    mover_river,
    mover_turn_price,
    mover_river_price,
    rival_turn,
    rival_river,
    rival_turn_price,
    rival_river_price,
):
    river_count = lax.axis_size("river")
    river_here = lax.axis_index("river")
    hand_here = lax.axis_index("hand")
    slots = mover_river.shape[0]
    sequences = mover_river.shape[1]
    infosets = mover_river_price.shape[1]
    width = mover_river.shape[2]
    total_count = (mover_turn.shape[0] + mover_turn_price.shape[0]) * H + river_count * slots * (
        sequences + infosets
    ) * H
    card_one, card_two = card_tables()
    own_one = lax.dynamic_slice_in_dim(card_one, hand_here * width, width)
    own_two = lax.dynamic_slice_in_dim(card_two, hand_here * width, width)
    deck = jnp.arange(CARDS, dtype=jnp.int32)
    own_cards = ((own_one[:, None] == deck[None, :]) | (own_two[:, None] == deck[None, :])).astype(
        jnp.float32
    )
    turn_all = turn_alive(card_one, card_two, turn_cards)
    turn_own = lax.dynamic_slice_in_dim(turn_all, hand_here * width, width)
    turn_step = (turn_children - turn_parents).astype(jnp.float32)
    turn_root = 1.0 - jnp.sum(turn_parents, axis=1).astype(jnp.float32)
    river_step = (river_children - river_parents[:, :sequences]).astype(jnp.float32)
    river_link = river_parents[:, sequences:].astype(jnp.float32)
    slot_used = (jnp.arange(slots) < loads[river_here]).astype(jnp.float32)
    live_own = (hand_rank >= 0).astype(jnp.float32) * slot_used[:, None] * turn_own[None, :]
    rank_all = lax.all_gather(hand_rank, "hand", axis=1, tiled=True)
    live_all = (rank_all >= 0).astype(jnp.float32) * slot_used[:, None] * turn_all[None, :]
    live_three = live_own[:, None, :]
    first_row = (river_here == 0).astype(jnp.float32)

    def turn_partial(plan):
        weighted = turn_own[None, :] * plan
        return (jnp.dot(weighted, own_cards, precision=HIGH), jnp.sum(weighted, axis=1))

    def turn_mixed(plan, card_sums, totals):
        near = jnp.dot(card_sums, own_cards.T, precision=HIGH)
        return turn_own[None, :] * (totals[:, None] - near + turn_own[None, :] * plan)

    def link_partial(mult):
        return jnp.einsum("qt,bqh->th", river_link, live_three * mult, precision=HIGH)

    def squares(turn_first, turn_second, river_first, river_second):
        turn_part = jnp.sum(turn_first * turn_first) + jnp.sum(turn_second * turn_second)
        return (
            first_row * turn_part
            + jnp.sum(river_first * river_first)
            + jnp.sum(river_second * river_second)
        )

    def shared_sums(mult, plan, norm_terms):
        link_local = link_partial(mult)
        card_local, total_local = turn_partial(plan)
        link = lax.psum(link_local, "river")
        card_sums, totals = lax.psum((card_local, total_local), "hand")
        norms = None
        if norm_terms is not None:
            norms = lax.psum(norm_terms, ("river", "hand"))
        return (link, card_sums, totals, norms)

    def river_payoff(plans, direction, pot_matrix, fold_matrix):
        boards = plans.shape[0]
        count = group_size(boards, 4)
        batch_blocks = jax.vmap(pair_blocks, in_axes=(0, 0, None, None, 0, 0, None, None, None))
        start_value = jnp.zeros((boards, 2, plans.shape[1], width), jnp.float32)
        piece = lax.all_gather(plans, "hand", axis=2, tiled=True)
        span = piece.shape[2]
        far_rank = lax.slice_in_dim(rank_all, 0, span, axis=1)
        far_live = lax.slice_in_dim(live_all, 0, span, axis=1)
        far_one = lax.slice_in_dim(card_one, 0, span, axis=0)
        far_two = lax.slice_in_dim(card_two, 0, span, axis=0)

        def per_group(args):
            plan_group, near_rank, near_live, rank_group, live_group = args
            blocks = batch_blocks(
                near_rank,
                near_live,
                own_one,
                own_two,
                rank_group,
                live_group,
                far_one,
                far_two,
                direction,
            )
            return jnp.einsum("btc,bkac->bkta", plan_group, blocks, precision=HIGH)

        parts = lax.map(
            per_group,
            (
                grouped(piece, count),
                grouped(hand_rank, count),
                grouped(live_own, count),
                grouped(far_rank, count),
                grouped(far_live, count),
            ),
        )
        mixed = start_value + parts.reshape(start_value.shape)
        return (
            jnp.einsum("st,bth->bsh", pot_matrix, mixed[:, 0], precision=HIGH)
            + jnp.einsum("st,bth->bsh", fold_matrix, mixed[:, 1], precision=HIGH)
        ) / H

    mover_turn = turn_own[None, :] * mover_turn
    mover_turn_price = turn_own[None, :] * mover_turn_price
    rival_turn = turn_own[None, :] * rival_turn
    rival_turn_price = turn_own[None, :] * rival_turn_price
    mover_river = live_three * mover_river
    mover_river_price = live_three * mover_river_price
    rival_river = live_three * rival_river
    rival_river_price = live_three * rival_river_price
    for step in range(ITERS):
        norm_terms = (
            squares(mover_turn, mover_turn_price, mover_river, mover_river_price),
            squares(rival_turn, rival_turn_price, rival_river, rival_river_price),
        )
        link, card_sums, totals, norms = shared_sums(rival_river_price, rival_turn, norm_terms)
        weight = jnp.sqrt((norms[1] / total_count + EPSILON) / (norms[0] / total_count + EPSILON))
        primal_step = STEP_SCALE / weight
        dual_step = STEP_SCALE * weight
        grad_turn = jnp.dot(
            turn_fold, turn_mixed(rival_turn, card_sums, totals), precision=HIGH
        ) / H + turn_own[None, :] * (jnp.dot(turn_step.T, rival_turn_price, precision=HIGH) - link)
        grad_river = river_payoff(
            rival_river, 1.0, showdown_pot, river_fold
        ) + live_three * jnp.einsum("qs,bqh->bsh", river_step, rival_river_price, precision=HIGH)
        new_turn = turn_own[None, :] * jnp.maximum(mover_turn - primal_step * grad_turn, 0.0)
        new_river = live_three * jnp.maximum(mover_river - primal_step * grad_river, 0.0)
        new_turn_price = mover_turn_price + primal_step * turn_own[None, :] * (
            jnp.dot(turn_step, rival_turn, precision=HIGH) - turn_root[:, None]
        )
        new_river_price = mover_river_price + primal_step * live_three * (
            jnp.einsum("qs,bsh->bqh", river_step, rival_river, precision=HIGH)
            - jnp.dot(river_link, rival_turn, precision=HIGH)[None]
        )
        turn_bar = 2.0 * new_turn - mover_turn
        river_bar = 2.0 * new_river - mover_river
        turn_price_bar = 2.0 * new_turn_price - mover_turn_price
        river_price_bar = 2.0 * new_river_price - mover_river_price
        mover_turn, mover_river, mover_turn_price, mover_river_price = (
            new_turn,
            new_river,
            new_turn_price,
            new_river_price,
        )
        link_bar, card_bar, totals_bar, unused = shared_sums(river_price_bar, turn_bar, None)
        rise_turn = jnp.dot(
            turn_fold.T, turn_mixed(turn_bar, card_bar, totals_bar), precision=HIGH
        ) / H - turn_own[None, :] * (
            jnp.dot(turn_step.T, turn_price_bar, precision=HIGH) - link_bar
        )
        rise_river = river_payoff(
            river_bar, -1.0, showdown_pot.T, river_fold.T
        ) - live_three * jnp.einsum("qs,bqh->bsh", river_step, river_price_bar, precision=HIGH)
        new_rival_turn = turn_own[None, :] * jnp.maximum(rival_turn + dual_step * rise_turn, 0.0)
        new_rival_river = live_three * jnp.maximum(rival_river + dual_step * rise_river, 0.0)
        rival_turn_price = rival_turn_price + dual_step * turn_own[None, :] * (
            jnp.dot(turn_step, turn_bar, precision=HIGH) - turn_root[:, None]
        )
        rival_river_price = rival_river_price + dual_step * live_three * (
            jnp.einsum("qs,bsh->bqh", river_step, river_bar, precision=HIGH)
            - jnp.dot(river_link, turn_bar, precision=HIGH)[None]
        )
        rival_turn, rival_river = (new_rival_turn, new_rival_river)
    return (
        mover_turn,
        mover_river,
        mover_turn_price,
        mover_river_price,
        rival_turn,
        rival_river,
        rival_turn_price,
        rival_river_price,
    )


def solution(mesh):
    placed = (
        P(("groups", "river"), "hand"),
        P("groups"),
        P("groups"),
        P(),
        P(),
        P(),
        P(),
        P(),
        P(),
        P(),
        P("groups", "hand"),
        P(("groups", "river"), None, "hand"),
        P("groups", "hand"),
        P(("groups", "river"), None, "hand"),
        P("groups", "hand"),
        P(("groups", "river"), None, "hand"),
        P("groups", "hand"),
        P(("groups", "river"), None, "hand"),
    )
    return jax.shard_map(
        local,
        mesh=mesh,
        in_specs=placed,
        out_specs=(
            P("groups", "hand"),
            P(("groups", "river"), None, "hand"),
            P("groups", "hand"),
            P(("groups", "river"), None, "hand"),
            P("groups", "hand"),
            P(("groups", "river"), None, "hand"),
            P("groups", "hand"),
            P(("groups", "river"), None, "hand"),
        ),
        check_vma=False,
    )
```

profile of v0, /device:TPU:0, one launch (start us, length us, event | category | flops | bytes accessed | tf_op | source)
XLA Modules:
  0.0 953.4 jit_solution(1664086579780586695)
XLA Ops:
  29.3 35.4 %all-reduce.1 = (f32[]{:T(128)}, f32[]{:T(128)}) all-reduce(f32[]{:T(128)S(6)} %add.182, f32[]{:T(128)S(6)} %add.186), channel_id=1, replica_groups=mesh['groups'=2,'river'=8,'hand'=2] {'river','hand'}, use_global_device_ids=true, to_apply=%region_5.0 | all-reduce | flops 2 | bytes 16 | tf_op jit(solution)/shard_map/psum | solution.py:131
  81.0 164.0 %while.44 = (s32[]{:T(128)}, f32[3,4,2,64,663]{4,3,1,0,2:T(8,128)}, s32[3,4,1326]{2,1,0:T(4,128)S(1)}, s32[3,4,663]{2,1,0:T(4,128)S(1)}, s32[663]{0:T(1024)S(1)}...) while((s32[]{:T(128)}, f32[3,4,2,64,663]{4,3,1,0,2:T(8,128)}, ...), condition=%wide.region_25.26_spmd.clone, body=%wide.region_24.25_spmd.sunk.clone.sunk | while | flops 5437468160 | bytes 71021016 | solution.py:161
  93.8 40.6 %fusion.236 = f32[1,4,2,64,663]{4,3,2,1,0:T(8,128)S(1)} fusion(f32[1,4,663,1326]{3,2,0,1:T(8,128)} %get-tuple-element.753, f32[1,4,663,1326]{3,2,0,1:T(8,128)} %get-tuple-element.754, f32[3,4,64,1326]{3,2,1,0:T(8,128)} %get-tuple-element.820, s32[]{:T(128)} %get-tuple-element.800), kind=kOutput, calls=%fused_computation.8.clone.1 | convolution fusion | flops 5408456704 | bytes 32717312 | tf_op jit(solution)/shard_map/while/body/eval_jaxpr/btc,bkac->bkta/dot_general | solution.py:159
  148.3 40.6 %fusion.236 = f32[1,4,2,64,663]{4,3,2,1,0:T(8,128)S(1)} fusion(f32[1,4,663,1326]{3,2,0,1:T(8,128)} %get-tuple-element.753, f32[1,4,663,1326]{3,2,0,1:T(8,128)} %get-tuple-element.754, f32[3,4,64,1326]{3,2,1,0:T(8,128)} %get-tuple-element.820, s32[]{:T(128)} %get-tuple-element.800), kind=kOutput, calls=%fused_computation.8.clone.1 | convolution fusion | flops 5408456704 | bytes 32717312 | tf_op jit(solution)/shard_map/while/body/eval_jaxpr/btc,bkac->bkta/dot_general | solution.py:159
  202.8 40.6 %fusion.236 = f32[1,4,2,64,663]{4,3,2,1,0:T(8,128)S(1)} fusion(f32[1,4,663,1326]{3,2,0,1:T(8,128)} %get-tuple-element.753, f32[1,4,663,1326]{3,2,0,1:T(8,128)} %get-tuple-element.754, f32[3,4,64,1326]{3,2,1,0:T(8,128)} %get-tuple-element.820, s32[]{:T(128)} %get-tuple-element.800), kind=kOutput, calls=%fused_computation.8.clone.1 | convolution fusion | flops 5408456704 | bytes 32717312 | tf_op jit(solution)/shard_map/while/body/eval_jaxpr/btc,bkac->bkta/dot_general | solution.py:159
  270.2 14.0 %all-gather.8.cloned.1.call-done = f32[12,64,1326]{1,0,2:T(8,128)} async-done(((f32[12,64,663]{1,0,2:T(8,128)}), f32[12,64,1326]{1,0,2:T(8,128)}) %all-gather.8.cloned.1.call-update) | async-done | bytes 4073488 | tf_op jit(solution)/shard_map/all_gather | solution.py:139
  296.6 164.3 %while.45 = (s32[]{:T(128)}, f32[3,4,2,64,663]{4,3,1,0,2:T(8,128)}, s32[3,4,1326]{2,1,0:T(4,128)S(1)}, s32[3,4,663]{2,1,0:T(4,128)S(1)}, s32[663]{0:T(1024)S(1)}...) while((s32[]{:T(128)}, f32[3,4,2,64,663]{4,3,1,0,2:T(8,128)}, ...), condition=%wide.region_27.28_spmd.clone, body=%wide.region_26.27_spmd.sunk.clone.sunk | while | flops 5440984576 | bytes 71021016 | solution.py:161
  298.4 11.1 %multiply_multiply_fusion.8 = (f32[1,4,663,1326]{3,2,0,1:T(8,128)}, f32[1,4,663,1326]{3,2,0,1:T(8,128)}) fusion(s32[4,663]{1,0:T(4,128)S(1)} %dynamic-slice_bitcast_fusion.36, s32[4,1326]{1,0:T(4,128)S(1)} %dynamic-slice_bitcast_fusion.37, f32[4,1326]{1,0:T(4,128)S(1)} %dynamic-slice_bitcast_fusion.38, f32[4,663]{1,0:T(4,128)S(1)} %dynamic-slice_bitcast_fusion.39, ...), kind=kLoop, calls=%fused_computation.22.clone.1 | loop fusion | flops 24615864 | bytes 31712616 | tf_op jit(solution)/shard_map/while/body/eval_jaxpr/vmap()/mul | solution.py:40
  309.5 40.6 %fusion.238 = f32[1,4,2,64,663]{4,3,2,1,0:T(8,128)S(1)} fusion(f32[1,4,663,1326]{3,2,0,1:T(8,128)} %get-tuple-element.764, f32[1,4,663,1326]{3,2,0,1:T(8,128)} %get-tuple-element.765, f32[3,4,64,1326]{3,2,1,0:T(8,128)} %get-tuple-element.856, s32[]{:T(128)} %get-tuple-element.836), kind=kOutput, calls=%fused_computation.25.clone.1 | convolution fusion | flops 5408456704 | bytes 32717312 | tf_op jit(solution)/shard_map/while/body/eval_jaxpr/btc,bkac->bkta/dot_general | solution.py:159
  352.9 11.1 %multiply_multiply_fusion.8 = (f32[1,4,663,1326]{3,2,0,1:T(8,128)}, f32[1,4,663,1326]{3,2,0,1:T(8,128)}) fusion(s32[4,663]{1,0:T(4,128)S(1)} %dynamic-slice_bitcast_fusion.36, s32[4,1326]{1,0:T(4,128)S(1)} %dynamic-slice_bitcast_fusion.37, f32[4,1326]{1,0:T(4,128)S(1)} %dynamic-slice_bitcast_fusion.38, f32[4,663]{1,0:T(4,128)S(1)} %dynamic-slice_bitcast_fusion.39, ...), kind=kLoop, calls=%fused_computation.22.clone.1 | loop fusion | flops 24615864 | bytes 31712616 | tf_op jit(solution)/shard_map/while/body/eval_jaxpr/vmap()/mul | solution.py:40
  364.0 40.6 %fusion.238 = f32[1,4,2,64,663]{4,3,2,1,0:T(8,128)S(1)} fusion(f32[1,4,663,1326]{3,2,0,1:T(8,128)} %get-tuple-element.764, f32[1,4,663,1326]{3,2,0,1:T(8,128)} %get-tuple-element.765, f32[3,4,64,1326]{3,2,1,0:T(8,128)} %get-tuple-element.856, s32[]{:T(128)} %get-tuple-element.836), kind=kOutput, calls=%fused_computation.25.clone.1 | convolution fusion | flops 5408456704 | bytes 32717312 | tf_op jit(solution)/shard_map/while/body/eval_jaxpr/btc,bkac->bkta/dot_general | solution.py:159
  407.5 11.1 %multiply_multiply_fusion.8 = (f32[1,4,663,1326]{3,2,0,1:T(8,128)}, f32[1,4,663,1326]{3,2,0,1:T(8,128)}) fusion(s32[4,663]{1,0:T(4,128)S(1)} %dynamic-slice_bitcast_fusion.36, s32[4,1326]{1,0:T(4,128)S(1)} %dynamic-slice_bitcast_fusion.37, f32[4,1326]{1,0:T(4,128)S(1)} %dynamic-slice_bitcast_fusion.38, f32[4,663]{1,0:T(4,128)S(1)} %dynamic-slice_bitcast_fusion.39, ...), kind=kLoop, calls=%fused_computation.22.clone.1 | loop fusion | flops 24615864 | bytes 31712616 | tf_op jit(solution)/shard_map/while/body/eval_jaxpr/vmap()/mul | solution.py:40
  418.6 40.6 %fusion.238 = f32[1,4,2,64,663]{4,3,2,1,0:T(8,128)S(1)} fusion(f32[1,4,663,1326]{3,2,0,1:T(8,128)} %get-tuple-element.764, f32[1,4,663,1326]{3,2,0,1:T(8,128)} %get-tuple-element.765, f32[3,4,64,1326]{3,2,1,0:T(8,128)} %get-tuple-element.856, s32[]{:T(128)} %get-tuple-element.836), kind=kOutput, calls=%fused_computation.25.clone.1 | convolution fusion | flops 5408456704 | bytes 32717312 | tf_op jit(solution)/shard_map/while/body/eval_jaxpr/btc,bkac->bkta/dot_general | solution.py:159
  502.7 34.4 %all-reduce = (f32[]{:T(128)}, f32[]{:T(128)}) all-reduce(f32[]{:T(128)S(6)} %add.202, f32[]{:T(128)S(6)} %add.206), channel_id=1, replica_groups=mesh['groups'=2,'river'=8,'hand'=2] {'river','hand'}, use_global_device_ids=true, to_apply=%region_30.31 | all-reduce | flops 2 | bytes 16 | tf_op jit(solution)/shard_map/psum | solution.py:131
  555.7 164.1 %while.46 = (s32[]{:T(128)}, f32[3,4,2,64,663]{4,3,1,0,2:T(8,128)}, s32[3,4,1326]{2,1,0:T(4,128)S(1)}, s32[3,4,663]{2,1,0:T(4,128)S(1)}, s32[663]{0:T(1024)S(1)}...) while((s32[]{:T(128)}, f32[3,4,2,64,663]{4,3,1,0,2:T(8,128)}, ...), condition=%wide.region_42.43_spmd.clone, body=%wide.region_41.42_spmd.sunk.clone.sunk | while | flops 5437468160 | bytes 71021016 | solution.py:161
  568.5 40.6 %fusion.240 = f32[1,4,2,64,663]{4,3,2,1,0:T(8,128)S(1)} fusion(f32[1,4,663,1326]{3,2,0,1:T(8,128)} %get-tuple-element.775, f32[1,4,663,1326]{3,2,0,1:T(8,128)} %get-tuple-element.776, f32[3,4,64,1326]{3,2,1,0:T(8,128)} %get-tuple-element.892, s32[]{:T(128)} %get-tuple-element.872), kind=kOutput, calls=%fused_computation.42.clone.1 | convolution fusion | flops 5408456704 | bytes 32717312 | tf_op jit(solution)/shard_map/while/body/eval_jaxpr/btc,bkac->bkta/dot_general | solution.py:159
  623.1 40.6 %fusion.240 = f32[1,4,2,64,663]{4,3,2,1,0:T(8,128)S(1)} fusion(f32[1,4,663,1326]{3,2,0,1:T(8,128)} %get-tuple-element.775, f32[1,4,663,1326]{3,2,0,1:T(8,128)} %get-tuple-element.776, f32[3,4,64,1326]{3,2,1,0:T(8,128)} %get-tuple-element.892, s32[]{:T(128)} %get-tuple-element.872), kind=kOutput, calls=%fused_computation.42.clone.1 | convolution fusion | flops 5408456704 | bytes 32717312 | tf_op jit(solution)/shard_map/while/body/eval_jaxpr/btc,bkac->bkta/dot_general | solution.py:159
  677.6 40.6 %fusion.240 = f32[1,4,2,64,663]{4,3,2,1,0:T(8,128)S(1)} fusion(f32[1,4,663,1326]{3,2,0,1:T(8,128)} %get-tuple-element.775, f32[1,4,663,1326]{3,2,0,1:T(8,128)} %get-tuple-element.776, f32[3,4,64,1326]{3,2,1,0:T(8,128)} %get-tuple-element.892, s32[]{:T(128)} %get-tuple-element.872), kind=kOutput, calls=%fused_computation.42.clone.1 | convolution fusion | flops 5408456704 | bytes 32717312 | tf_op jit(solution)/shard_map/while/body/eval_jaxpr/btc,bkac->bkta/dot_general | solution.py:159
  770.0 164.1 %while.47 = (s32[]{:T(128)}, f32[3,4,2,64,663]{4,3,1,0,2:T(8,128)}, s32[3,4,1326]{2,1,0:T(4,128)S(1)}, s32[3,4,663]{2,1,0:T(4,128)S(1)}, s32[663]{0:T(1024)S(1)}...) while((s32[]{:T(128)}, f32[3,4,2,64,663]{4,3,1,0,2:T(8,128)}, ...), condition=%wide.region_49.50_spmd.clone, body=%wide.region_48.49_spmd.sunk.clone.sunk | while | flops 5440984576 | bytes 71021016 | solution.py:161
  771.8 11.1 %multiply_multiply_fusion.9 = (f32[1,4,663,1326]{3,2,0,1:T(8,128)}, f32[1,4,663,1326]{3,2,0,1:T(8,128)}) fusion(s32[4,663]{1,0:T(4,128)S(1)} %dynamic-slice_bitcast_fusion.44, s32[4,1326]{1,0:T(4,128)S(1)} %dynamic-slice_bitcast_fusion.45, f32[4,1326]{1,0:T(4,128)S(1)} %dynamic-slice_bitcast_fusion.46, f32[4,663]{1,0:T(4,128)S(1)} %dynamic-slice_bitcast_fusion.47, ...), kind=kLoop, calls=%fused_computation.56.clone.1 | loop fusion | flops 24615864 | bytes 31712616 | tf_op jit(solution)/shard_map/while/body/eval_jaxpr/vmap()/mul | solution.py:40
  782.9 40.6 %fusion.242 = f32[1,4,2,64,663]{4,3,2,1,0:T(8,128)S(1)} fusion(f32[1,4,663,1326]{3,2,0,1:T(8,128)} %get-tuple-element.786, f32[1,4,663,1326]{3,2,0,1:T(8,128)} %get-tuple-element.787, f32[3,4,64,1326]{3,2,1,0:T(8,128)} %get-tuple-element.928, s32[]{:T(128)} %get-tuple-element.908), kind=kOutput, calls=%fused_computation.59.clone.1 | convolution fusion | flops 5408456704 | bytes 32717312 | tf_op jit(solution)/shard_map/while/body/eval_jaxpr/btc,bkac->bkta/dot_general | solution.py:159
  826.3 11.1 %multiply_multiply_fusion.9 = (f32[1,4,663,1326]{3,2,0,1:T(8,128)}, f32[1,4,663,1326]{3,2,0,1:T(8,128)}) fusion(s32[4,663]{1,0:T(4,128)S(1)} %dynamic-slice_bitcast_fusion.44, s32[4,1326]{1,0:T(4,128)S(1)} %dynamic-slice_bitcast_fusion.45, f32[4,1326]{1,0:T(4,128)S(1)} %dynamic-slice_bitcast_fusion.46, f32[4,663]{1,0:T(4,128)S(1)} %dynamic-slice_bitcast_fusion.47, ...), kind=kLoop, calls=%fused_computation.56.clone.1 | loop fusion | flops 24615864 | bytes 31712616 | tf_op jit(solution)/shard_map/while/body/eval_jaxpr/vmap()/mul | solution.py:40
  837.4 40.6 %fusion.242 = f32[1,4,2,64,663]{4,3,2,1,0:T(8,128)S(1)} fusion(f32[1,4,663,1326]{3,2,0,1:T(8,128)} %get-tuple-element.786, f32[1,4,663,1326]{3,2,0,1:T(8,128)} %get-tuple-element.787, f32[3,4,64,1326]{3,2,1,0:T(8,128)} %get-tuple-element.928, s32[]{:T(128)} %get-tuple-element.908), kind=kOutput, calls=%fused_computation.59.clone.1 | convolution fusion | flops 5408456704 | bytes 32717312 | tf_op jit(solution)/shard_map/while/body/eval_jaxpr/btc,bkac->bkta/dot_general | solution.py:159
  892.0 40.6 %fusion.242 = f32[1,4,2,64,663]{4,3,2,1,0:T(8,128)S(1)} fusion(f32[1,4,663,1326]{3,2,0,1:T(8,128)} %get-tuple-element.786, f32[1,4,663,1326]{3,2,0,1:T(8,128)} %get-tuple-element.787, f32[3,4,64,1326]{3,2,1,0:T(8,128)} %get-tuple-element.928, s32[]{:T(128)} %get-tuple-element.908), kind=kOutput, calls=%fused_computation.59.clone.1 | convolution fusion | flops 5408456704 | bytes 32717312 | tf_op jit(solution)/shard_map/while/body/eval_jaxpr/btc,bkac->bkta/dot_general | solution.py:159
  (261 shorter events, 295.5 us)
Async XLA Ops:
  8.0 237.1 %copy-start = (f32[64,64]{1,0:T(8,128)S(1)}, f32[64,64]{1,0:T(8,128)}, u32[]{:S(2)}) copy-start(f32[64,64]{1,0:T(8,128)} %param.36) | copy-start | bytes 49156
  8.0 60.6 %all-gather.6.cloned.1.call-start = ((), (), s32[]{:S(2)}) async-start(), calls=%async_computation | async-start | bytes 16293888 | tf_op jit(solution)/shard_map/all_gather | solution.py:139
  8.9 59.5 %copy-start.28 = (f32[1326]{0:T(1024)}, f32[1326]{0:T(1024)S(1)}, u32[]{:S(2)}) copy-start(f32[1326]{0:T(1024)S(1)} %convert_subtract_fusion.4) | copy-start | bytes 15916
  10.8 253.1 %copy-start.32 = (f32[12]{0:T(128)}, f32[12]{0:T(128)S(1)}, u32[]{:S(2)}) copy-start(f32[12]{0:T(128)S(1)} %compare_convert_fusion) | copy-start | bytes 148
  11.8 252.1 %copy-start.27 = (pred[12,663]{1,0:T(8,128)(4,1)}, pred[12,663]{1,0:T(8,128)(4,1)S(1)}, u32[]{:S(2)}) copy-start(pred[12,663]{1,0:T(8,128)(4,1)S(1)} %get-tuple-element.513) | copy-start | bytes 23872
  15.4 249.2 %copy-start.3 = (f32[12,64,663]{2,1,0:T(8,128)}, f32[12,64,663]{2,1,0:T(8,128)S(1)}, u32[]{:S(2)}) copy-start(f32[12,64,663]{2,1,0:T(8,128)S(1)} %get-tuple-element.511) | copy-start | bytes 6110212
  20.2 44.6 %copy-start.14 = (s32[1326]{0:T(1024)S(1)}, s32[1326]{0:T(1024)}, u32[]{:S(2)}) copy-start(s32[1326]{0:T(1024)} %constant.126.clone) | copy-start | bytes 15916
  20.2 44.7 %copy-start.15 = (s32[1326]{0:T(1024)S(1)}, s32[1326]{0:T(1024)}, u32[]{:S(2)}) copy-start(s32[1326]{0:T(1024)} %constant.127.clone) | copy-start | bytes 15916
  20.2 44.7 %copy-start.20 = (s32[12,663]{1,0:T(8,128)S(1)}, s32[12,663]{1,0:T(8,128)}, u32[]{:S(2)}) copy-start(s32[12,663]{1,0:T(8,128)} %param.28) | copy-start | bytes 95476
  20.2 48.4 %copy-start.18 = (s32[16,80]{1,0:T(8,128)S(1)}, s32[16,80]{1,0:T(8,128)}, u32[]{:S(2)}) copy-start(s32[16,80]{1,0:T(8,128)} %param.34) | copy-start | bytes 15364
  20.2 48.4 %copy-start.34 = (s32[16,64]{1,0:T(8,128)S(1)}, s32[16,64]{1,0:T(8,128)}, u32[]{:S(2)}) copy-start(s32[16,64]{1,0:T(8,128)} %param.33) | copy-start | bytes 12292
  20.3 264.0 %all-gather.8.cloned.1.call-start = ((), (), s32[]{:S(2)}) async-start(), calls=%async_computation.1 | async-start | bytes 16293888 | tf_op jit(solution)/shard_map/all_gather | solution.py:139
  263.6 218.8 %all-reduce.13.cloned.1.call-start = ((), (), s32[]{:S(2)}) async-start(), calls=%async_computation.5 | async-start | bytes 196608 | tf_op jit(solution)/shard_map/psum | solution.py:127
  267.7 271.6 %copy-start.6 = (f32[12,16,663]{2,1,0:T(8,128)}, f32[12,16,663]{2,1,0:T(8,128)S(1)}, u32[]{:S(2)}) copy-start(f32[12,16,663]{2,1,0:T(8,128)S(1)} %get-tuple-element.536) | copy-start | bytes 1527556
  269.6 273.7 %all-gather.10.cloned.1.call-start = ((), (), s32[]{:S(2)}) async-start(), calls=%async_computation.2 | async-start | bytes 16293888 | tf_op jit(solution)/shard_map/all_gather | solution.py:139
  472.2 67.1 %copy-start.1 = (f32[12,64,663]{2,1,0:T(8,128)}, f32[12,64,663]{2,1,0:T(8,128)S(1)}, u32[]{:S(2)}) copy-start(f32[12,64,663]{2,1,0:T(8,128)S(1)} %get-tuple-element.544) | copy-start | bytes 6110212
  477.1 266.9 %all-reduce.11.cloned.1.call-start = ((), (), s32[]{:S(2)}) async-start(), calls=%async_computation.4 | async-start | bytes 196608 | tf_op jit(solution)/shard_map/psum | solution.py:127
  480.3 8.9 copy-start.33
  543.3 214.4 %all-gather.12.cloned.1.call-start = ((), (), s32[]{:S(2)}) async-start(), calls=%async_computation.3 | async-start | bytes 16293888 | tf_op jit(solution)/shard_map/all_gather | solution.py:139
  719.8 8.1 copy-start.9
  719.8 8.1 copy-start.10
  744.0 23.4 %copy-start.31 = (f32[6,663]{1,0:T(8,128)}, f32[6,663]{1,0:T(8,128)S(1)}, u32[]{:S(2)}) copy-start(f32[6,663]{1,0:T(8,128)S(1)} %fusion.99) | copy-start | bytes 47740
  934.1 7.9 copy-start.2
  934.1 7.9 copy-start.7
  (21 other events, 87.4 us)
Sparse Core Ops, SparseCore 0:
  20.4 25.9 all-gather.5
  263.7 20.4 all-gather.7
  477.2 24.3 all-gather.9
  737.0 20.4 all-gather.11
Sparse Core Ops, SparseCore 1:
  269.7 66.6 all-reduce.12
  543.3 66.6 all-reduce.10
where the time goes:
time: 959 us; the launch traced here: 953 us
  matrix products  572 us (60%)
  other arithmetic  163 us (17%)
  local copies, waits for them, and re-layouts  89.4 us (9%)
  blocking collectives  83 us (9%)
  between operations  29.3 us (3%)
  waiting for transfers between devices  14.2 us (1%)
    dot_general x12, matrix products, per_group(): return jnp.einsum('btc,bkac->bkta', plan_group, blocks, precision=HIGH)  487 us
    mul x12, other arithmetic, pair_blocks(): return jnp.stack([signs * indicator, indicator])  133 us
    psum x2, blocking collectives, shared_sums(): norms = lax.psum(norm_terms, ('river', 'hand'))  69.9 us
    all_gather x4, local copies, waits for them, and re-layouts, river_payoff(): piece = lax.all_gather(plans, 'hand', axis=2, tiled=True)  38.8 us
  transfers between devices with their start and end apart: 6, of which 1 were waited for; matrix products, arithmetic and copies ran while one was open for 45% of the time, Pallas kernels for 0%

commit v1 on v0

v1 whole, which is shorter than its diff:
```python
import functools

import jax
import jax.numpy as jnp
import ml_dtypes
import numpy as np
from jax import lax
from jax.experimental import pallas as pl
from jax.experimental.pallas import tpu as pltpu
from jax.sharding import PartitionSpec as P

CARDS = 52
H = 1326
ITERS = 2
STEP_SCALE = 0.25
EPSILON = 1e-06
HIGH = lax.Precision.HIGHEST
LANES = 128
TILE = 256
VMEM_BYTES = 56 * 2**20
F32 = jnp.float32
BF16 = jnp.bfloat16


def round_up(value, unit):
    return -(-value // unit) * unit


def halves(width, padded):
    pairs = np.stack(np.triu_indices(CARDS, 1)).astype(np.int32)
    deck = np.arange(CARDS)
    incidence = (pairs[0][:, None] == deck) | (pairs[1][:, None] == deck)
    parts = pairs.shape[1] // width
    cards = np.full((parts, 8, 2 * padded), -1, np.int32)
    compat = np.zeros((parts, 2 * padded, padded), np.float32)
    gather = np.zeros((parts, 2 * padded, LANES), np.float32)
    spread = np.zeros((parts, LANES, 2 * padded), np.float32)
    for part in range(parts):
        own = slice(part * width, (part + 1) * width)
        for place, half in enumerate((part, 1 - part)):
            far = slice(half * width, (half + 1) * width)
            rows = slice(place * padded, place * padded + width)
            cards[part, :2, rows] = pairs[:, far]
            shared = incidence[far].astype(np.int32) @ incidence[own].T.astype(np.int32)
            compat[part, rows, :width] = shared == 0
            compat[part, rows, width:width + CARDS] = incidence[far]
            compat[part, rows, width + CARDS] = 1.0
            gather[part, rows, :CARDS] = incidence[far]
            gather[part, rows, CARDS] = 1.0
            spread[part, :CARDS, rows] = -incidence[far].T.astype(np.float32)
            spread[part, CARDS, rows] = 1.0
    near = np.zeros((parts, LANES, padded), np.float32)
    first = width - (padded - LANES)
    near[:, first:first + CARDS + 1] = spread[:, :CARDS + 1, :padded]
    exact = ml_dtypes.bfloat16
    return (cards, compat.astype(exact), gather.astype(exact), spread.astype(exact), near.astype(exact))


def split_two(value):
    high = value.astype(BF16)
    return high, (value - high.astype(F32)).astype(BF16)


def exact_right(value, matrix):
    rows = value.shape[0]
    first = value.astype(BF16)
    rest = value - first.astype(F32)
    second = rest.astype(BF16)
    third = (rest - second.astype(F32)).astype(BF16)
    total = jnp.dot(jnp.concatenate([first, second, third], axis=0), matrix, preferred_element_type=F32)
    return total[:rows] + total[rows:2 * rows] + total[2 * rows:]


def full_dot(left, right):
    return jnp.dot(left, right, precision=HIGH, preferred_element_type=F32)


def alive_rows(card_rows, turn_cards):
    one, two = card_rows[0:1], card_rows[1:2]
    held = one < 0
    for place in range(4):
        card = turn_cards[place]
        held = held | (one == card) | (two == card)
    return jnp.where(held, 0.0, 1.0).astype(F32)


def lane_sums(value):
    total = jnp.sum(value, axis=0, keepdims=True)
    parts = [total[:, at:at + LANES] for at in range(0, total.shape[1], LANES)]
    return functools.reduce(jnp.add, parts)


def steps_from(norms, count):
    totals = jnp.sum(norms, axis=1, keepdims=True)
    weight = jnp.sqrt((totals[1:2] / count + EPSILON) / (totals[0:1] / count + EPSILON))
    return STEP_SCALE / weight, STEP_SCALE * weight


def fetch_steps(norms_ref, count, step_scratch):
    primal, dual = steps_from(norms_ref[...], count)
    step_scratch[0:1, :] = jnp.broadcast_to(primal, (1, LANES))
    step_scratch[1:2, :] = jnp.broadcast_to(dual, (1, LANES))


def river_steps(children_ref, parents_ref):
    sequences = children_ref.shape[1]
    step = (children_ref[...] - parents_ref[:, :sequences]).astype(F32)
    return step, parents_ref[:, sequences:].astype(F32)


def stats_kernel(slots, group, river_axis, loads_ref, cards_now_ref, card_ref, rank_ref, x_ref, v_ref, y_ref, u_ref,
                 xt_ref, vt_ref, yt_ref, ut_ref, children_ref, parents_ref,
                 sums_ref, pack_ref, norms_ref, live_scratch, plan_scratch):
    at = pl.program_id(0)
    padded = live_scratch.shape[2]
    prices = v_ref.shape[1]
    river_here = lax.axis_index(river_axis)

    @pl.when(at == 0)
    def _():
        turn = alive_rows(card_ref[0, :, :padded], cards_now_ref)
        slot = lax.broadcasted_iota(jnp.int32, (slots, padded), 0)
        rank = rank_ref[...]
        live = jnp.where((rank >= 0) & (slot < loads_ref[river_here]) & (turn > 0), 1.0, 0.0)
        for board in range(slots):
            live_scratch[board] = live[board:board + 1]
        sums_ref[...] = jnp.zeros_like(sums_ref)
        plan_scratch[...] = jnp.zeros_like(plan_scratch)
        pack_ref[...] = jnp.zeros_like(pack_ref)
        norms_ref[...] = jnp.zeros_like(norms_ref)
        first = jnp.where(river_here == 0, 1.0, 0.0)
        base = 0
        for rows, row in ((xt_ref, 0), (vt_ref, 0), (yt_ref, 1), (ut_ref, 1)):
            value = jnp.where(turn > 0, rows[...], 0.0)
            pack_ref[base:base + value.shape[0]] = value
            base += round_up(value.shape[0], 8)
            norms_ref[row:row + 1] += first * lane_sums(value * value)

    nx = jnp.zeros((1, LANES), F32)
    ny = jnp.zeros((1, LANES), F32)
    for inner in range(group):
        live = live_scratch[at * group + inner] > 0
        x = jnp.where(live, x_ref[inner], 0.0)
        v = jnp.where(live, v_ref[inner], 0.0)
        y = jnp.where(live, y_ref[inner], 0.0)
        u = jnp.where(live, u_ref[inner], 0.0)
        nx = nx + lane_sums(x * x) + lane_sums(v * v)
        ny = ny + lane_sums(y * y) + lane_sums(u * u)
        sums_ref[0:prices] += u
        sums_ref[prices:2 * prices] += v
        plan_scratch[...] += y
    norms_ref[0:1] += nx
    norms_ref[1:2] += ny

    @pl.when(at == pl.num_programs(0) - 1)
    def _():
        step, _ = river_steps(children_ref, parents_ref)
        sums_ref[2 * prices:3 * prices] = full_dot(step, plan_scratch[...])


def rank_kernel(slots, group, river_axis, loads_ref, cards_now_ref, card_ref, own_ref, far_ref, live_ref, row_ref, col_ref):
    padded = row_ref.shape[2]
    rank = jnp.concatenate([own_ref[...], far_ref[...]], axis=1)
    turn = alive_rows(card_ref[0], cards_now_ref)
    slot = lax.broadcasted_iota(jnp.int32, rank.shape, 0)
    live = jnp.where((rank >= 0) & (slot < loads_ref[lax.axis_index(river_axis)]) & (turn > 0), 1.0, 0.0)
    safe = jnp.where(live > 0, rank, 0)
    code = (128 + (safe & 127)).astype(F32)
    high = safe >> 7
    for bit in range(6):
        code = code * jnp.where((high >> bit) & 1 == 1, float(2.0 ** (1 << bit)), 1.0)
    lane = lax.broadcasted_iota(jnp.int32, rank.shape, 1)
    width = H // (2 * padded // padded)
    own_code = jnp.where(lane[:, :padded] < width, code[:, :padded], 0.0)
    for board in range(slots):
        live_ref[board] = live[board:board + 1]
        row_ref[board] = own_code[board:board + 1].astype(BF16)
    depth = round_up(slots, 8)
    if depth > slots:
        code = jnp.concatenate([code, jnp.zeros((depth - slots, code.shape[1]), F32)], axis=0)
    turned = code.T
    for place in range(slots // group):
        col_ref[place] = turned[:, place * group:(place + 1) * group]


def set_operators(transposed, pot_ref, fold_ref, children_ref, parents_ref, main_scratch, fold_scratch, back_scratch):
    pot = pot_ref[...] / H
    fold = fold_ref[...] / H
    if transposed:
        pot, fold = -pot.T, fold.T
    step, _ = river_steps(children_ref, parents_ref)
    sequences = pot.shape[0]
    infosets = step.shape[0]
    pot_high, pot_low = split_two(pot)
    fold_high, fold_low = split_two(fold)
    main_scratch[:sequences] = jnp.concatenate([pot_high, pot_high, fold_high, fold_high], axis=1)
    main_scratch[sequences:2 * sequences] = jnp.concatenate([pot_low, pot_low, fold_low, fold_low], axis=1)
    exact = step.astype(BF16)
    main_scratch[2 * sequences:2 * sequences + infosets] = jnp.concatenate(
        [jnp.zeros((infosets, 2 * sequences), BF16), exact, exact], axis=1)
    fold_scratch[:sequences] = jnp.concatenate([fold_high, fold_high], axis=1)
    fold_scratch[sequences:] = jnp.concatenate([fold_low, fold_low], axis=1)
    turned = step.T
    if transposed:
        turned = -turned
    turned = turned.astype(BF16)
    back_scratch[...] = jnp.concatenate([turned, turned], axis=1)


def payoffs(own_plans, far_plans, prices, col_ref, row_ref, compat_ref, near_ref, main_scratch, fold_scratch, back_scratch):
    sequences, padded = own_plans[0].shape
    tiles = padded // TILE
    results = []
    cards = []
    for inner in range(len(own_plans)):
        own_high, own_low = split_two(own_plans[inner])
        far_high, far_low = split_two(far_plans[inner])
        left = (jnp.concatenate([own_high, own_low], axis=0), jnp.concatenate([far_high, far_low], axis=0))
        row = row_ref[inner]
        sums = [None] * tiles
        for place in range(2 * tiles):
            rows = slice(place * TILE, (place + 1) * TILE)
            column = jnp.broadcast_to(col_ref[0, rows, inner:inner + 1], (TILE, LANES)).astype(BF16)
            column = jnp.concatenate([column, column], axis=1)
            piece = left[place // tiles][:, (place % tiles) * TILE:(place % tiles + 1) * TILE]
            for across in range(tiles):
                lanes = slice(across * TILE, (across + 1) * TILE)
                bound = compat_ref[0, rows, lanes]
                signs = jnp.minimum(jnp.maximum(column - row[:, lanes], -bound), bound)
                part = jnp.dot(piece, signs, preferred_element_type=F32)
                sums[across] = part if sums[across] is None else sums[across] + part
        mixed = jnp.concatenate(sums, axis=1)
        mixed = mixed[:sequences] + mixed[sequences:]
        mixed_high, mixed_low = split_two(mixed)
        stacked = jnp.concatenate([mixed_high, mixed_low, own_high, own_low], axis=0)
        main = jnp.dot(main_scratch[...], stacked, preferred_element_type=F32)
        price_high, price_low = split_two(prices[inner])
        back = jnp.dot(back_scratch[...], jnp.concatenate([price_high, price_low], axis=0), preferred_element_type=F32)
        tail = jnp.concatenate([mixed_high[:, padded - LANES:], mixed_low[:, padded - LANES:]], axis=0)
        folded = jnp.dot(fold_scratch[...], tail, preferred_element_type=F32)
        cards.extend(split_two(folded[:sequences] + folded[sequences:]))
        results.append((main[:sequences] + main[sequences:2 * sequences] + back, main[2 * sequences:]))
    nearby = jnp.dot(jnp.concatenate(cards, axis=0), near_ref[0], preferred_element_type=F32)
    done = []
    for inner, (gradient, flow) in enumerate(results):
        base = 2 * inner * sequences
        close = nearby[base:base + sequences] + nearby[base + sequences:base + 2 * sequences]
        done.append((gradient + close, flow))
    return done


def mover_gradient_kernel(group, hand_ref, y_ref, far_ref, u_ref, live_ref, col_ref, row_ref, compat_ref, near_ref,
                          yt_ref, pot_ref, fold_ref, children_ref, parents_ref,
                          grad_ref, flow_ref, main_scratch, fold_scratch, back_scratch, link_scratch):
    padded = grad_ref.shape[2]

    @pl.when(pl.program_id(0) == 0)
    def _():
        set_operators(False, pot_ref, fold_ref, children_ref, parents_ref, main_scratch, fold_scratch, back_scratch)
        _, link = river_steps(children_ref, parents_ref)
        link_scratch[...] = full_dot(link, yt_ref[...])

    own_plans, far_plans, prices, lives = [], [], [], []
    for inner in range(group):
        live = live_ref[inner]
        lives.append(live[:, :padded])
        own_plans.append(jnp.where(live[:, :padded] > 0, y_ref[inner], 0.0))
        far_plans.append(jnp.where(live[:, padded:] > 0, far_ref[inner], 0.0))
        prices.append(jnp.where(live[:, :padded] > 0, u_ref[inner], 0.0))
    done = payoffs(own_plans, far_plans, prices, col_ref, row_ref, compat_ref, near_ref, main_scratch, fold_scratch, back_scratch)
    for inner, (gradient, flow) in enumerate(done):
        grad_ref[inner] = gradient
        flow_ref[inner] = lives[inner] * (flow - link_scratch[...])


def mover_step_kernel(group, count, last, norms_ref, x_ref, v_ref, grad_ref, flow_ref, live_ref, children_ref, parents_ref,
                      new_x_ref, new_v_ref, bar_ref, *rest):
    at = pl.program_id(0)
    padded = bar_ref.shape[2]
    step_scratch = rest[-1]
    if not last:
        sum_ref, out_norms_ref, plan_scratch, _ = rest

    @pl.when(at == 0)
    def _():
        fetch_steps(norms_ref, count, step_scratch)
        if not last:
            plan_scratch[...] = jnp.zeros_like(plan_scratch)
            out_norms_ref[...] = jnp.zeros_like(out_norms_ref)

    primal = step_scratch[0:1, 0:1]
    for inner in range(group):
        live = live_ref[inner][:, :padded]
        x = jnp.where(live > 0, x_ref[inner], 0.0)
        v = jnp.where(live > 0, v_ref[inner], 0.0)
        new_x = live * jnp.maximum(x - primal * grad_ref[inner], 0.0)
        new_v = v + primal * flow_ref[inner]
        bar = 2.0 * new_x - x
        new_x_ref[inner] = new_x
        new_v_ref[inner] = new_v
        bar_ref[inner] = bar
        if not last:
            plan_scratch[...] += bar
            out_norms_ref[0:1] += lane_sums(new_x * new_x) + lane_sums(new_v * new_v)

    if not last:
        @pl.when(at == pl.num_programs(0) - 1)
        def _():
            step, _ = river_steps(children_ref, parents_ref)
            sum_ref[...] = full_dot(step, plan_scratch[...])


def rival_step_kernel(group, count, last, hand_ref, norms_ref, bar_ref, far_ref, y_ref, u_ref, new_v_ref, flow_ref, live_ref,
                      col_ref, row_ref, compat_ref, near_ref, bart_ref, pot_ref, fold_ref, children_ref, parents_ref, *rest):
    at = pl.program_id(0)
    if last:
        new_y_ref, new_u_ref, main_scratch, fold_scratch, back_scratch, link_scratch, step_scratch = rest
    else:
        (part_ref, new_y_ref, new_u_ref, sum_ref, out_norms_ref, main_scratch, fold_scratch, back_scratch, link_scratch,
         step_scratch, plan_scratch) = rest
    padded = live_ref.shape[2] // 2

    @pl.when(at == 0)
    def _():
        fetch_steps(norms_ref, count, step_scratch)
        set_operators(True, pot_ref, fold_ref, children_ref, parents_ref, main_scratch, fold_scratch, back_scratch)
        _, link = river_steps(children_ref, parents_ref)
        link_scratch[...] = full_dot(link, bart_ref[...])
        if not last:
            plan_scratch[...] = jnp.zeros_like(plan_scratch)
            out_norms_ref[...] = part_ref[...]

    primal = step_scratch[0:1, 0:1]
    dual = step_scratch[1:2, 0:1]
    own_plans, far_plans, prices = [], [], []
    for inner in range(group):
        own_plans.append(bar_ref[inner])
        far_plans.append(far_ref[inner])
        prices.append(new_v_ref[inner] + primal * flow_ref[inner])
    done = payoffs(own_plans, far_plans, prices, col_ref, row_ref, compat_ref, near_ref, main_scratch, fold_scratch, back_scratch)
    for inner, (gradient, flow) in enumerate(done):
        live = live_ref[inner][:, :padded]
        y = jnp.where(live > 0, y_ref[inner], 0.0)
        u = jnp.where(live > 0, u_ref[inner], 0.0)
        new_y = live * jnp.maximum(y + dual * gradient, 0.0)
        new_u = u + dual * (live * (flow - link_scratch[...]))
        new_y_ref[inner] = new_y
        new_u_ref[inner] = new_u
        if not last:
            plan_scratch[...] += new_y
            out_norms_ref[1:2] += lane_sums(new_y * new_y) + lane_sums(new_u * new_u)

    if not last:
        @pl.when(at == pl.num_programs(0) - 1)
        def _():
            step, _ = river_steps(children_ref, parents_ref)
            sum_ref[...] = full_dot(step, plan_scratch[...])


def turn_step_kernel(count, first, names, hand_ref, cards_now_ref, card_ref, gather_ref, spread_ref, norms_ref, *rest):
    if first:
        own_ref, far_ref, sums_ref, sums_far_ref = rest[:4]
        rest = rest[4:]
    else:
        pack_ref, kept_ref, old_bar_ref, old_norms_ref, sums_ref, sums_far_ref = rest[:6]
        rest = rest[6:]
    turn_fold_ref, turn_children_ref, turn_parents_ref, children_ref, parents_ref = rest[:5]
    rest = rest[5:]
    primal, dual = steps_from(norms_ref[...], count)
    turn = alive_rows(card_ref[0], cards_now_ref)
    _, link = river_steps(children_ref, parents_ref)
    link_turned = link.T
    parents = turn_parents_ref[...].astype(F32)
    turn_step = turn_children_ref[...].astype(F32) - parents
    turn_root = 1.0 - jnp.sum(parents, axis=1, keepdims=True)
    step_turned = turn_step.T
    fold = turn_fold_ref[...]
    meetings = (CARDS - 6) * turn
    sequences = fold.shape[0]
    points = turn_step.shape[0]
    slab = round_up(points, 8)
    starts = (0, sequences, sequences + slab, 2 * sequences + slab)
    infosets = link.shape[0]
    sums = jnp.concatenate([sums_ref[...], sums_far_ref[...]], axis=1)
    if first:
        pack = jnp.concatenate([own_ref[...], far_ref[...]], axis=1)
        price_sum = sums[:infosets]
        kept = sums[infosets:2 * infosets]
        plan_sum = sums[2 * infosets:]
    else:
        pack = pack_ref[...]
        _, old_dual = steps_from(old_norms_ref[...], count)
        price_sum = kept_ref[:infosets] + old_dual * (
            sums[:infosets] - meetings * full_dot(link, old_bar_ref[...]))
        kept = kept_ref[infosets:]
        plan_sum = sums[infosets:]
    x = pack[starts[0]:starts[0] + sequences]
    v = pack[starts[1]:starts[1] + points]
    y = pack[starts[2]:starts[2] + sequences]
    u = pack[starts[3]:starts[3] + points]

    def mix(plan):
        return turn * (exact_right(exact_right(plan, gather_ref[0]), spread_ref[0]) + plan)

    grad = full_dot(fold, mix(y)) / H + turn * (full_dot(step_turned, u) - full_dot(link_turned, price_sum))
    new_x = turn * jnp.maximum(x - primal * grad, 0.0)
    new_v = v + primal * (turn * (full_dot(turn_step, y) - turn_root))
    bar = 2.0 * new_x - x
    price_bar = 2.0 * new_v - v
    drift = primal * (plan_sum - meetings * full_dot(link, y))
    rise = full_dot(fold.T, mix(bar)) / H - turn * (
        full_dot(step_turned, price_bar) - full_dot(link_turned, kept + 2.0 * drift))
    new_y = turn * jnp.maximum(y + dual * rise, 0.0)
    new_u = u + dual * (turn * (full_dot(turn_step, bar) - turn_root))
    if first:
        out_pack_ref, out_kept_ref, bar_ref, out_norms_ref = rest
        out_pack_ref[...] = jnp.zeros_like(out_pack_ref)
        for start, value in zip(starts, (new_x, new_v, new_y, new_u)):
            out_pack_ref[start:start + value.shape[0]] = value
        out_kept_ref[:infosets] = price_sum
        out_kept_ref[infosets:] = kept + drift
        bar_ref[...] = bar
        river_name, hand_name = names
        flag = jnp.where((lax.axis_index(river_name) == 0) & (hand_ref[0] == 0), 1.0, 0.0)
        out_norms_ref[...] = jnp.zeros_like(out_norms_ref)
        out_norms_ref[0:1] = flag * (lane_sums(new_x * new_x) + lane_sums(new_v * new_v))
        out_norms_ref[1:2] = flag * (lane_sums(new_y * new_y) + lane_sums(new_u * new_u))
    else:
        bar_ref = rest[0]
        bar_ref[...] = bar
        for out_ref, value in zip(rest[1:], (new_x, new_v, new_y, new_u)):
            out_ref[...] = value[:, :out_ref.shape[1]]


def whole(shape):
    return pl.BlockSpec(shape, lambda *at: (0,) * len(shape))


def smem():
    return pl.BlockSpec(memory_space=pltpu.SMEM)


def local(hand_rank, loads, turn_cards, turn_children, turn_parents, river_children, river_parents, showdown_pot, river_fold,
          turn_fold, mover_turn, mover_river, mover_turn_price, mover_river_price, rival_turn, rival_river,
          rival_turn_price, rival_river_price):
    slots, sequences, width = mover_river.shape
    infosets = mover_river_price.shape[1]
    turn_sequences = mover_turn.shape[0]
    points = mover_turn_price.shape[0]
    river_count = lax.axis_size("river")
    padded = round_up(width + CARDS + 1, TILE)
    count = float((turn_sequences + points) * H + river_count * slots * (sequences + infosets) * H)
    group = next(size for size in (3, 2, 1) if slots % size == 0)
    grid = (slots // group,)
    cards, compat, gather, spread, near = (jnp.asarray(table) for table in halves(width, padded))
    hand = lax.axis_index("hand").astype(jnp.int32).reshape(1)
    pack_rows = 2 * (turn_sequences + round_up(points, 8))
    params = pltpu.CompilerParams(vmem_limit_bytes=VMEM_BYTES)

    def shape(*dims, dtype=F32):
        return jax.ShapeDtypeStruct(dims, dtype)

    def swap(value):
        return lax.ppermute(value, "hand", [(0, 1), (1, 0)])

    def river_total(value):
        if river_count & (river_count - 1):
            return lax.psum(value, "river")
        hop = 1
        while hop < river_count:
            value = value + lax.ppermute(value, "river", [(at, at ^ hop) for at in range(river_count)])
            hop *= 2
        return value

    def boards(rows):
        return pl.BlockSpec((group, rows, padded), lambda at, *_: (at, 0, 0))

    live_block = pl.BlockSpec((group, 1, 2 * padded), lambda at, *_: (at, 0, 0))
    col_block = pl.BlockSpec((1, 2 * padded, group), lambda at, *_: (at, 0, 0))
    row_block = pl.BlockSpec((group, 1, padded), lambda at, *_: (at, 0, 0))
    compat_block = pl.BlockSpec((1, 2 * padded, padded), lambda at, ref: (ref[0], 0, 0))
    near_block = pl.BlockSpec((1, LANES, padded), lambda at, ref: (ref[0], 0, 0))
    card_block = pl.BlockSpec((1, 8, 2 * padded), lambda at, ref: (ref[0], 0, 0))
    tree_blocks = [whole(river_children.shape), whole(river_parents.shape)]
    half_block = lambda rows: pl.BlockSpec((rows, padded), lambda at, *_: (0, 0))
    norm_block = whole((8, LANES))
    operator_scratch = [pltpu.VMEM((2 * sequences + infosets, 4 * sequences), BF16),
                        pltpu.VMEM((2 * sequences, 2 * sequences), BF16),
                        pltpu.VMEM((sequences, 2 * infosets), BF16),
                        pltpu.VMEM((infosets, padded), F32)]
    step_scratch = pltpu.VMEM((8, LANES), F32)
    plan_scratch = pltpu.VMEM((sequences, padded), F32)

    rank_far = swap(hand_rank)
    rival_far = swap(rival_river)

    def stats_call(*args):
        def kernel(hand_ref, *refs):
            stats_kernel(slots, group, "river", *refs)
        return pl.pallas_call(
            kernel,
            grid_spec=pltpu.PrefetchScalarGridSpec(
                num_scalar_prefetch=1, grid=grid,
                in_specs=[smem(), smem(), card_block, half_block(slots), boards(sequences), boards(infosets),
                          boards(sequences), boards(infosets), half_block(turn_sequences), half_block(points),
                          half_block(turn_sequences), half_block(points)] + tree_blocks,
                out_specs=[whole((3 * infosets, padded)), whole((pack_rows, padded)), norm_block],
                scratch_shapes=[pltpu.VMEM((slots, 1, padded), F32), plan_scratch]),
            out_shape=[shape(3 * infosets, padded), shape(pack_rows, padded), shape(8, LANES)],
            compiler_params=params, name="stats",
        )(hand, *args)

    sums, pack, norms = stats_call(
        loads, turn_cards, cards, hand_rank, mover_river, mover_river_price, rival_river, rival_river_price,
        mover_turn, mover_turn_price, rival_turn, rival_turn_price, river_children, river_parents)

    norms = norms + swap(norms)
    norms = river_total(norms)
    pack_far = swap(pack)
    sums = river_total(sums)
    sums_far = swap(sums)

    def rank_call(*args):
        def kernel(hand_ref, *refs):
            rank_kernel(slots, group, "river", *refs)
        return pl.pallas_call(
            kernel,
            grid_spec=pltpu.PrefetchScalarGridSpec(
                num_scalar_prefetch=1, grid=(1,),
                in_specs=[smem(), smem(), card_block, half_block(slots), half_block(slots)],
                out_specs=[whole((slots, 1, 2 * padded)), whole((slots, 1, padded)), whole((slots // group, 2 * padded, group))]),
            out_shape=[shape(slots, 1, 2 * padded), shape(slots, 1, padded, dtype=BF16), shape(slots // group, 2 * padded, group)],
            compiler_params=params, name="ranks",
        )(hand, *args)

    live, rows, cols = rank_call(loads, turn_cards, cards, hand_rank, rank_far)
    board_blocks = [live_block, col_block, row_block, compat_block, near_block]
    board_tables = (live, cols, rows, compat, near)
    matrix_blocks = [whole(showdown_pot.shape), whole(river_fold.shape)] + tree_blocks
    matrices = (showdown_pot, river_fold, river_children, river_parents)

    def gradient_call(y, y_far, u, y_turn):
        return pl.pallas_call(
            functools.partial(mover_gradient_kernel, group),
            grid_spec=pltpu.PrefetchScalarGridSpec(
                num_scalar_prefetch=1, grid=grid,
                in_specs=[boards(sequences), boards(sequences), boards(infosets)] + board_blocks
                + [half_block(turn_sequences)] + matrix_blocks,
                out_specs=[boards(sequences), boards(infosets)],
                scratch_shapes=operator_scratch),
            out_shape=[shape(slots, sequences, padded), shape(slots, infosets, padded)],
            compiler_params=params, name="mover_gradient",
        )(hand, y, y_far, u, *board_tables, y_turn, *matrices)

    def mover_call(last, norms, x, v, grad, flow):
        out_width = width if last else padded
        out_specs = [boards(sequences), boards(infosets), boards(sequences)]
        out_shape = [shape(slots, sequences, out_width), shape(slots, infosets, out_width), shape(slots, sequences, padded)]
        scratch = [step_scratch]
        if not last:
            out_specs += [whole((infosets, padded)), norm_block]
            out_shape += [shape(infosets, padded), shape(8, LANES)]
            scratch = [plan_scratch, step_scratch]
        return pl.pallas_call(
            functools.partial(mover_step_kernel, group, count, last),
            grid_spec=pltpu.PrefetchScalarGridSpec(
                num_scalar_prefetch=0, grid=grid,
                in_specs=[norm_block, boards(sequences), boards(infosets), boards(sequences), boards(infosets), live_block] + tree_blocks,
                out_specs=out_specs, scratch_shapes=scratch),
            out_shape=out_shape, compiler_params=params, name="mover_step",
        )(norms, x, v, grad, flow, live, river_children, river_parents)

    def rival_call(last, norms, bar, bar_far, y, u, new_v, flow, bar_turn, part):
        out_width = width if last else padded
        in_specs = [norm_block, boards(sequences), boards(sequences), boards(sequences), boards(infosets), boards(infosets),
                    boards(infosets)] + board_blocks + [half_block(turn_sequences)] + matrix_blocks
        out_specs = [boards(sequences), boards(infosets)]
        out_shape = [shape(slots, sequences, out_width), shape(slots, infosets, out_width)]
        scratch = operator_scratch + [step_scratch]
        args = (hand, norms, bar, bar_far, y, u, new_v, flow, *board_tables, bar_turn, *matrices)
        if not last:
            in_specs.append(norm_block)
            out_specs += [whole((infosets, padded)), norm_block]
            out_shape += [shape(infosets, padded), shape(8, LANES)]
            scratch = scratch + [plan_scratch]
            args = args + (part,)
        return pl.pallas_call(
            functools.partial(rival_step_kernel, group, count, last),
            grid_spec=pltpu.PrefetchScalarGridSpec(
                num_scalar_prefetch=1, grid=grid, in_specs=in_specs, out_specs=out_specs, scratch_shapes=scratch),
            out_shape=out_shape, compiler_params=params, name="rival_step",
        )(*args)

    both = 2 * padded
    turn_blocks = [smem(), card_block, pl.BlockSpec((1, both, LANES), lambda at, ref: (ref[0], 0, 0)),
                   pl.BlockSpec((1, LANES, both), lambda at, ref: (ref[0], 0, 0)), norm_block]
    turn_tables = (turn_cards, cards, gather, spread)
    turn_matrix_blocks = [whole(turn_fold.shape), whole(turn_children.shape), whole(turn_parents.shape)] + tree_blocks
    turn_matrices = (turn_fold, turn_children, turn_parents, river_children, river_parents)

    def turn_call(first, norms, data):
        if first:
            in_data = [whole((pack_rows, padded))] * 2 + [whole((3 * infosets, padded))] * 2
            out_shape = [shape(pack_rows, both), shape(2 * infosets, both), shape(turn_sequences, both), shape(8, LANES)]
        else:
            in_data = [whole((pack_rows, both)), whole((2 * infosets, both)), whole((turn_sequences, both)), norm_block] + [
                whole((2 * infosets, padded))] * 2
            out_shape = [shape(turn_sequences, both), shape(turn_sequences, width), shape(points, width),
                         shape(turn_sequences, width), shape(points, width)]
        return pl.pallas_call(
            functools.partial(turn_step_kernel, count, first, ("river", "hand")),
            grid_spec=pltpu.PrefetchScalarGridSpec(
                num_scalar_prefetch=1, grid=(1,), in_specs=turn_blocks + in_data + turn_matrix_blocks,
                out_specs=[whole(item.shape) for item in out_shape]),
            out_shape=out_shape, compiler_params=params, name="turn_step",
        )(hand, *turn_tables, norms, *data, *turn_matrices)

    y_start = turn_sequences + round_up(points, 8)
    grad, flow = gradient_call(rival_river, rival_far, rival_river_price, lax.slice_in_dim(pack, y_start, y_start + turn_sequences))
    x, v, bar, bar_sum, part = mover_call(False, norms, mover_river, mover_river_price, grad, flow)
    bar_far = swap(bar)
    pack, kept, bar_turn, turn_norms = turn_call(True, norms, (pack, pack_far, sums, sums_far))
    y, u, plan_sum, part = rival_call(False, norms, bar, bar_far, rival_river, rival_river_price, v, flow, bar_turn,
                                      part + turn_norms)
    y_far = swap(y)
    next_norms = river_total(part + swap(part))
    sums = river_total(jnp.concatenate([bar_sum, plan_sum], axis=0))
    sums_far = swap(sums)
    grad, flow = gradient_call(y, y_far, u, lax.slice_in_dim(pack, y_start, y_start + turn_sequences))
    next_x, next_v, bar = mover_call(True, next_norms, x, v, grad, flow)
    bar_far = swap(bar)
    bar_turn, next_xt, next_vt, next_yt, next_ut = turn_call(
        False, next_norms, (pack, kept, bar_turn, norms, sums, sums_far))
    next_y, next_u = rival_call(True, next_norms, bar, bar_far, y, u, next_v, flow, bar_turn, None)
    return (next_xt, next_x, next_vt, next_v, next_yt, next_y, next_ut, next_u)


def solution(mesh):
    river = P(("groups", "river"), None, "hand")
    turn = P("groups", "hand")
    placed = (P(("groups", "river"), "hand"), P("groups"), P("groups"), P(), P(), P(), P(), P(), P(), P(),
              turn, river, turn, river, turn, river, turn, river)
    return jax.shard_map(local, mesh=mesh, in_specs=placed,
                         out_specs=(turn, river, turn, river, turn, river, turn, river), check_vma=False)
```

time: 959 us -> 176 us (0.18)
  matrix products: 572 us -> 0 us
  other arithmetic: 163 us -> 3.96 us
  Pallas kernels: 0 us -> 91.4 us
  blocking collectives: 83 us -> 0 us
  local copies, waits for them, and re-layouts: 89.4 us -> 10.6 us
  waiting for transfers between devices: 14.2 us -> 43.2 us
  between operations: 29.3 us -> 1.01 us
  starting transfers between devices: 0.25 us -> 25.3 us
    dot_general x56 -> x0, matrix products: 572 us -> none  [the longest x12 487 us: per_group(): return jnp.einsum('btc,bkac->bkta', plan_group, blocks, precision=HIGH)]
    mul x18 -> x0, other arithmetic: 136 us -> none  [the longest x12 133 us: pair_blocks(): return jnp.stack([signs * indicator, indicator])]
    pallas_call x0 -> x10, Pallas kernels: none -> 91.4 us  [the longest x2 32 us: rival_call(): pl.pallas_call(functools.partial(rival_step_kernel, group, count, last),...]
    psum x6 -> x0, blocking collectives: 81.1 us -> none  [the longest x2 69.9 us: shared_sums(): norms = lax.psum(norm_terms, ('river', 'hand'))]
    ppermute x0 -> x22, waiting for transfers between devices: none -> 43.2 us  [the longest x12 35.3 us: river_total(): lax.ppermute(value, 'river', [(at, at ^ hop) for at in range(river_count)])]
    all_gather x5 -> x0, local copies, waits for them, and re-layouts: 38.9 us -> none  [the longest x4 38.8 us: river_payoff(): piece = lax.all_gather(plans, 'hand', axis=2, tiled=True)]
    ppermute x0 -> x22, starting transfers between devices: none -> 25.3 us  [the longest x12 23.4 us: river_total(): lax.ppermute(value, 'river', [(at, at ^ hop) for at in range(river_count)])]
    sub x15 -> x0, other arithmetic: 18.3 us -> none  [the longest x12 18.3 us: pair_blocks(): 1.0 - shared.astype(jnp.float32)]
  transfers between devices with their start and end apart: 6 -> 22, of which waited for: 1 -> 16; matrix products, arithmetic and copies ran while one was open for 45% -> 4% of each run, Pallas kernels for 0% -> 9%
where the time goes in v1:
time: 176 us; the launch traced here: 175 us
  Pallas kernels  91.4 us (52%)
  waiting for transfers between devices  43.2 us (25%)
  starting transfers between devices  25.3 us (14%)
  local copies, waits for them, and re-layouts  10.6 us (6%)
  other arithmetic  3.96 us (2%)
    ppermute x12, waiting for transfers between devices, river_total(): lax.ppermute(value, 'river', [(at, at ^ hop) for at in range(river_count)])  35.3 us
    pallas_call x2, Pallas kernels, rival_call(): pl.pallas_call(functools.partial(rival_step_kernel, group, count, last),...  32 us
    pallas_call x2, Pallas kernels, gradient_call(): pl.pallas_call(functools.partial(mover_gradient_kernel, group), grid_spec...  30.8 us
    ppermute x12, starting transfers between devices, river_total(): lax.ppermute(value, 'river', [(at, at ^ hop) for at in range(river_count)])  23.4 us
    pallas_call x2, Pallas kernels, mover_call(): pl.pallas_call(functools.partial(mover_step_kernel, group, count, last),...  12.5 us
    ppermute x10, waiting for transfers between devices, swap(): return lax.ppermute(value, 'hand', [(0, 1), (1, 0)])  7.91 us
    unnamed x31, local copies, waits for them, and re-layouts  7.66 us
    pallas_call x2, Pallas kernels, turn_call(): pl.pallas_call(functools.partial(turn_step_kernel, count, first, ('river'...  7.65 us
  transfers between devices with their start and end apart: 22, of which 16 were waited for; matrix products, arithmetic and copies ran while one was open for 4% of the time, Pallas kernels for 9%

profile of v1, /device:TPU:0, one launch (start us, length us, event | category | flops | bytes accessed | tf_op | source)
XLA Modules:
  0.0 175.5 jit_solution(2757844722046897175)
XLA Ops:
  1.2 4.9 %stats.1 = (f32[48,768]{1,0:T(8,128)}, f32[48,768]{1,0:T(8,128)}, f32[8,128]{1,0:T(8,128)}) custom-call(s32[1]{0:T(128)} %bitcast.hand_ref, s32[8]{0:T(128)} %refs_0_.3, s32[4]{0:T(128)} %cards_now_ref.3, s32[2,8,1536]{2,1,0:T(8,128)} %constant.14.clone.refs_2_.card_ref, s32[12,663]{1,0:T(8,128)} %refs_3_.3, f32[12,64,663]{2,1,0:T(8,128)} %x_ref.1, ...), custom_call_target="tpu_custom_call" | custom-call | tf_op jit(solution)/shard_map/stats/pallas_call | solution.py:500
  8.4 2.9 %collective-permute-start.1 = (f32[8,128]{1,0:T(8,128)S(1)}, f32[8,128]{1,0:T(8,128)S(1)}, u32[]{:S(2)}, u32[]{:S(2)}) collective-permute-start(f32[8,128]{1,0:T(8,128)S(1)} %add.45), channel_id=1, source_target_pairs={{0,2},{2,0},{4,6},{6,4},{8,10},{10,8},{12,14},{14,12},{1,3},{3,1},... | collective-permute-start | bytes 12296 | tf_op jit(solution)/shard_map/ppermute | solution.py:471
  12.8 2.1 %collective-permute-start.2 = (f32[8,128]{1,0:T(8,128)S(1)}, f32[8,128]{1,0:T(8,128)S(1)}, u32[]{:S(2)}, u32[]{:S(2)}) collective-permute-start(f32[8,128]{1,0:T(8,128)S(1)} %add.46), channel_id=1, source_target_pairs={{0,4},{2,6},{4,0},{6,2},{8,12},{10,14},{12,8},{14,10},{1,5},{3,7},... | collective-permute-start | bytes 12296 | tf_op jit(solution)/shard_map/ppermute | solution.py:471
  16.5 3.0 %collective-permute-start.3 = (f32[8,128]{1,0:T(8,128)S(1)}, f32[8,128]{1,0:T(8,128)S(1)}, u32[]{:S(2)}, u32[]{:S(2)}) collective-permute-start(f32[8,128]{1,0:T(8,128)S(1)} %add.47), channel_id=1, source_target_pairs={{0,8},{2,10},{4,12},{6,14},{8,0},{10,2},{12,4},{14,6},{1,9},{3,11}... | collective-permute-start | bytes 12296 | tf_op jit(solution)/shard_map/ppermute | solution.py:471
  22.4 3.4 %ranks.1 = (f32[12,1,1536]{2,1,0:T(1,128)}, bf16[12,1,768]{2,1,0:T(2,128)(2,1)}, f32[4,1536,3]{2,1,0:T(8,128)}) custom-call(s32[1]{0:T(128)} %bitcast.hand_ref, s32[8]{0:T(128)} %refs_0_.3, s32[4]{0:T(128)} %cards_now_ref.3, s32[2,8,1536]{2,1,0:T(8,128)} %constant.14.clone.refs_2_.card_ref, s32[12,663]{1,0:T(8,128)} %refs_3_.3, s32[12,663]{1,0:T(8,128)} %copy-done.13), custom_call_target="tpu_custom_call" | custom-call | tf_op jit(solution)/shard_map/ranks/pallas_call | solution.py:526
  27.2 15.3 %mover_gradient.2 = (f32[12,64,768]{2,1,0:T(8,128)}, f32[12,16,768]{2,1,0:T(8,128)}) custom-call(s32[1]{0:T(128)} %bitcast.hand_ref, f32[12,64,663]{2,1,0:T(8,128)} %y_ref.3, f32[12,64,663]{2,1,0:T(8,128)} %copy-done.1, f32[12,16,663]{2,1,0:T(8,128)} %u_ref.3, f32[12,1,1536]{2,1,0:T(1,128)} %get-tuple-element.42.live_ref, ...), custom_call_target="tpu_custom_call" | custom-call | tf_op jit(solution)/shard_map/mover_gradient/pallas_call | solution.py:543
  42.5 6.7 %mover_step.2 = (f32[12,64,768]{2,1,0:T(8,128)}, f32[12,16,768]{2,1,0:T(8,128)}, f32[12,64,768]{2,1,0:T(8,128)}, f32[16,768]{1,0:T(8,128)}, f32[8,128]{1,0:T(8,128)}) custom-call(f32[8,128]{1,0:T(8,128)} %add.48.norms_ref.rest_3_, f32[12,64,663]{2,1,0:T(8,128)} %x_ref.1, f32[12,16,663]{2,1,0:T(8,128)} %v_ref.1, f32[12,64,768]{2,1,0:T(8,128)} %get-tuple-element.46.grad_ref, ...), custom_call_target="tpu_custom_call" | custom-call | tf_op jit(solution)/shard_map/mover_step/pallas_call | solution.py:564
  51.2 4.4 %collective-permute-done.8 = f32[48,768]{1,0:T(8,128)S(1)} collective-permute-done((f32[48,768]{1,0:T(8,128)S(1)}, f32[48,768]{1,0:T(8,128)S(1)}, u32[]{:S(2)}, u32[]{:S(2)}) %collective-permute-start.8) | collective-permute-done | bytes 147488 | tf_op jit(solution)/shard_map/ppermute | solution.py:471
  57.5 3.7 %collective-permute-done.9 = f32[48,768]{1,0:T(8,128)S(1)} collective-permute-done((f32[48,768]{1,0:T(8,128)S(1)}, f32[48,768]{1,0:T(8,128)S(1)}, u32[]{:S(2)}, u32[]{:S(2)}) %collective-permute-start.9) | collective-permute-done | bytes 147488 | tf_op jit(solution)/shard_map/ppermute | solution.py:471
  61.3 2.8 %collective-permute-start.10 = (f32[48,768]{1,0:T(8,128)S(1)}, f32[48,768]{1,0:T(8,128)S(1)}, u32[]{:S(2)}, u32[]{:S(2)}) collective-permute-start(f32[48,768]{1,0:T(8,128)S(1)} %add.50), channel_id=1, source_target_pairs={{0,8},{2,10},{4,12},{6,14},{8,0},{10,2},{12,4},{14,6},{1,9},{3,11}... | collective-permute-start | bytes 442376 | tf_op jit(solution)/shard_map/ppermute | solution.py:471
  64.0 6.0 %collective-permute-done.10 = f32[48,768]{1,0:T(8,128)S(1)} collective-permute-done((f32[48,768]{1,0:T(8,128)S(1)}, f32[48,768]{1,0:T(8,128)S(1)}, u32[]{:S(2)}, u32[]{:S(2)}) %collective-permute-start.10) | collective-permute-done | bytes 147488 | tf_op jit(solution)/shard_map/ppermute | solution.py:471
  72.2 4.0 %turn_step.2 = (f32[48,1536]{1,0:T(8,128)}, f32[32,1536]{1,0:T(8,128)}, f32[16,1536]{1,0:T(8,128)}, f32[8,128]{1,0:T(8,128)}) custom-call(s32[1]{0:T(128)} %bitcast.hand_ref, s32[4]{0:T(128)} %cards_now_ref.3, s32[2,8,1536]{2,1,0:T(8,128)} %constant.14.clone.refs_2_.card_ref, bf16[2,1536,128]{2,1,0:T(8,128)(2,1)} %constant.16.clone.gather_ref, ...), custom_call_target="tpu_custom_call" | custom-call | tf_op jit(solution)/shard_map/turn_step/pallas_call | solution.py:610
  78.8 16.2 %rival_step.2 = (f32[12,64,768]{2,1,0:T(8,128)}, f32[12,16,768]{2,1,0:T(8,128)}, f32[16,768]{1,0:T(8,128)}, f32[8,128]{1,0:T(8,128)}) custom-call(s32[1]{0:T(128)} %bitcast.hand_ref, f32[8,128]{1,0:T(8,128)} %add.48.norms_ref.rest_3_, f32[12,64,768]{2,1,0:T(8,128)} %get-tuple-element.48.bar_ref, f32[12,64,768]{2,1,0:T(8,128)} %copy-done.2, ...), custom_call_target="tpu_custom_call" | custom-call | tf_op jit(solution)/shard_map/rival_step/pallas_call | solution.py:587
  95.6 4.2 %collective-permute-done.12 = f32[8,128]{1,0:T(8,128)S(1)} collective-permute-done((f32[8,128]{1,0:T(8,128)}, f32[8,128]{1,0:T(8,128)S(1)}, u32[]{:S(2)}, u32[]{:S(2)}) %collective-permute-start.12) | collective-permute-done | bytes 4128 | tf_op jit(solution)/shard_map/ppermute | solution.py:464
  102.1 2.1 %collective-permute-done.13 = f32[8,128]{1,0:T(8,128)S(1)} collective-permute-done((f32[8,128]{1,0:T(8,128)S(1)}, f32[8,128]{1,0:T(8,128)S(1)}, u32[]{:S(2)}, u32[]{:S(2)}) %collective-permute-start.13) | collective-permute-done | bytes 4128 | tf_op jit(solution)/shard_map/ppermute | solution.py:471
  104.8 3.0 %collective-permute-done.14 = f32[8,128]{1,0:T(8,128)S(1)} collective-permute-done((f32[8,128]{1,0:T(8,128)S(1)}, f32[8,128]{1,0:T(8,128)S(1)}, u32[]{:S(2)}, u32[]{:S(2)}) %collective-permute-start.14) | collective-permute-done | bytes 4128 | tf_op jit(solution)/shard_map/ppermute | solution.py:471
  114.3 15.5 %mover_gradient.3 = (f32[12,64,768]{2,1,0:T(8,128)}, f32[12,16,768]{2,1,0:T(8,128)}) custom-call(s32[1]{0:T(128)} %bitcast.hand_ref, f32[12,64,768]{2,1,0:T(8,128)} %get-tuple-element.61.y_ref, f32[12,64,768]{2,1,0:T(8,128)} %copy-done.3, f32[12,16,768]{2,1,0:T(8,128)} %get-tuple-element.62.u_ref, f32[12,1,1536]{2,1,0:T(1,128)} %get-tuple-element.42.live_ref, ...), custom_call_target="tpu_custom_call" | custom-call | tf_op jit(solution)/shard_map/mover_gradient/pallas_call | solution.py:543
  129.8 5.9 %mover_step.3 = (f32[12,64,663]{2,1,0:T(8,128)}, f32[12,16,663]{2,1,0:T(8,128)}, f32[12,64,768]{2,1,0:T(8,128)}) custom-call(f32[8,128]{1,0:T(8,128)} %add.56.norms_ref, f32[12,64,768]{2,1,0:T(8,128)} %get-tuple-element.60.x_ref, f32[12,16,768]{2,1,0:T(8,128)} %get-tuple-element.49.new_v_ref.v_ref, f32[12,64,768]{2,1,0:T(8,128)} %get-tuple-element.63.grad_ref, ...), custom_call_target="tpu_custom_call" | custom-call | tf_op jit(solution)/shard_map/mover_step/pallas_call | solution.py:564
  137.3 3.7 %collective-permute-done.16 = f32[32,768]{1,0:T(8,128)S(1)} collective-permute-done((f32[32,768]{1,0:T(8,128)S(1)}, f32[32,768]{1,0:T(8,128)S(1)}, u32[]{:S(2)}, u32[]{:S(2)}) %collective-permute-start.16) | collective-permute-done | bytes 98336 | tf_op jit(solution)/shard_map/ppermute | solution.py:471
  142.1 3.6 %collective-permute-done.17 = f32[32,768]{1,0:T(8,128)S(1)} collective-permute-done((f32[32,768]{1,0:T(8,128)S(1)}, f32[32,768]{1,0:T(8,128)S(1)}, u32[]{:S(2)}, u32[]{:S(2)}) %collective-permute-start.17) | collective-permute-done | bytes 98336 | tf_op jit(solution)/shard_map/ppermute | solution.py:471
  145.7 2.1 %collective-permute-start.18 = (f32[32,768]{1,0:T(8,128)S(1)}, f32[32,768]{1,0:T(8,128)S(1)}, u32[]{:S(2)}, u32[]{:S(2)}) collective-permute-start(f32[32,768]{1,0:T(8,128)S(1)} %add.58), channel_id=1, source_target_pairs={{0,8},{2,10},{4,12},{6,14},{8,0},{10,2},{12,4},{14,6},{1,9},{3,11}... | collective-permute-start | bytes 294920 | tf_op jit(solution)/shard_map/ppermute | solution.py:471
  147.8 4.5 %collective-permute-done.18 = f32[32,768]{1,0:T(8,128)S(1)} collective-permute-done((f32[32,768]{1,0:T(8,128)S(1)}, f32[32,768]{1,0:T(8,128)S(1)}, u32[]{:S(2)}, u32[]{:S(2)}) %collective-permute-start.18) | collective-permute-done | bytes 98336 | tf_op jit(solution)/shard_map/ppermute | solution.py:471
  154.4 3.7 %turn_step.3 = (f32[16,1536]{1,0:T(8,128)}, f32[16,663]{1,0:T(8,128)}, f32[6,663]{1,0:T(8,128)}, f32[16,663]{1,0:T(8,128)}, f32[6,663]{1,0:T(8,128)}) custom-call(s32[1]{0:T(128)} %bitcast.hand_ref, s32[4]{0:T(128)} %cards_now_ref.3, s32[2,8,1536]{2,1,0:T(8,128)} %constant.14.clone.refs_2_.card_ref, bf16[2,1536,128]{2,1,0:T(8,128)(2,1)} %constant.16.clone.gather_ref, ...), custom_call_target="tpu_custom_call" | custom-call | tf_op jit(solution)/shard_map/turn_step/pallas_call | solution.py:610
  159.6 15.8 %rival_step.3 = (f32[12,64,663]{2,1,0:T(8,128)}, f32[12,16,663]{2,1,0:T(8,128)}) custom-call(s32[1]{0:T(128)} %bitcast.hand_ref, f32[8,128]{1,0:T(8,128)} %add.56.norms_ref, f32[12,64,768]{2,1,0:T(8,128)} %get-tuple-element.69.bar_ref, f32[12,64,768]{2,1,0:T(8,128)} %copy-done, f32[12,64,768]{2,1,0:T(8,128)} %get-tuple-element.61.y_ref, ...), custom_call_target="tpu_custom_call" | custom-call | tf_op jit(solution)/shard_map/rival_step/pallas_call | solution.py:587
  (79 shorter events, 35.1 us)
Async XLA Ops:
  0.6 25.2 %collective-permute-start.4 = (f32[12,64,663]{2,1,0:T(8,128)}, f32[12,64,663]{2,1,0:T(8,128)S(1)}, u32[]{:S(2)}, u32[]{:S(2)}) collective-permute-start(f32[12,64,663]{2,1,0:T(8,128)} %y_ref.3), channel_id=1, source_target_pairs={{0,1},{1,0},{2,3},{3,2},{4,5},{5,4},{6,7},{7,6},{8,9},{9,8},{10,11... | collective-permute-start | bytes 6110216 | tf_op jit(solution)/shard_map/ppermute | solution.py:464
  1.2 20.6 %collective-permute-start.5 = (s32[12,663]{1,0:T(8,128)}, s32[12,663]{1,0:T(8,128)S(1)}, u32[]{:S(2)}, u32[]{:S(2)}) collective-permute-start(s32[12,663]{1,0:T(8,128)} %refs_3_.3), channel_id=1, source_target_pairs={{0,1},{1,0},{2,3},{3,2},{4,5},{5,4},{6,7},{7,6},{8,9},{9,8},{10,11... | collective-permute-start | bytes 95480 | tf_op jit(solution)/shard_map/ppermute | solution.py:464
  6.2 1.5 collective-permute-start
  8.4 4.4 %collective-permute-start.1 = (f32[8,128]{1,0:T(8,128)S(1)}, f32[8,128]{1,0:T(8,128)S(1)}, u32[]{:S(2)}, u32[]{:S(2)}) collective-permute-start(f32[8,128]{1,0:T(8,128)S(1)} %add.45), channel_id=1, source_target_pairs={{0,2},{2,0},{4,6},{6,4},{8,10},{10,8},{12,14},{14,12},{1,3},{3,1},... | collective-permute-start | bytes 12296 | tf_op jit(solution)/shard_map/ppermute | solution.py:471
  12.8 3.7 %collective-permute-start.2 = (f32[8,128]{1,0:T(8,128)S(1)}, f32[8,128]{1,0:T(8,128)S(1)}, u32[]{:S(2)}, u32[]{:S(2)}) collective-permute-start(f32[8,128]{1,0:T(8,128)S(1)} %add.46), channel_id=1, source_target_pairs={{0,4},{2,6},{4,0},{6,2},{8,12},{10,14},{12,8},{14,10},{1,5},{3,7},... | collective-permute-start | bytes 12296 | tf_op jit(solution)/shard_map/ppermute | solution.py:471
  16.5 4.6 %collective-permute-start.3 = (f32[8,128]{1,0:T(8,128)S(1)}, f32[8,128]{1,0:T(8,128)S(1)}, u32[]{:S(2)}, u32[]{:S(2)}) collective-permute-start(f32[8,128]{1,0:T(8,128)S(1)} %add.47), channel_id=1, source_target_pairs={{0,8},{2,10},{4,12},{6,14},{8,0},{10,2},{12,4},{14,6},{1,9},{3,11}... | collective-permute-start | bytes 12296 | tf_op jit(solution)/shard_map/ppermute | solution.py:471
  42.5 21.6 %copy-start.6 = (f32[48,768]{1,0:T(8,128)S(1)}, f32[48,768]{1,0:T(8,128)}, u32[]{:S(2)}) copy-start(f32[48,768]{1,0:T(8,128)} %get-tuple-element.45.rest_0_) | copy-start | bytes 442372
  49.2 26.9 %copy-start.14 = (f32[8,128]{1,0:T(8,128)S(1)}, f32[8,128]{1,0:T(8,128)}, u32[]{:S(2)}) copy-start(f32[8,128]{1,0:T(8,128)} %get-tuple-element.52) | copy-start | bytes 12292
  49.2 28.2 %collective-permute-start.6 = (f32[12,64,768]{2,1,0:T(8,128)}, f32[12,64,768]{2,1,0:T(8,128)S(1)}, u32[]{:S(2)}, u32[]{:S(2)}) collective-permute-start(f32[12,64,768]{2,1,0:T(8,128)} %get-tuple-element.48.bar_ref), channel_id=1, source_target_pairs={{0,1},{1,0},{2,3},{3,2},{4,5},{5,4},{6,7},{7,6},{8,9},{9,8},{10,11... | collective-permute-start | bytes 7077896 | tf_op jit(solution)/shard_map/ppermute | solution.py:464
  49.3 6.4 %collective-permute-start.8 = (f32[48,768]{1,0:T(8,128)S(1)}, f32[48,768]{1,0:T(8,128)S(1)}, u32[]{:S(2)}, u32[]{:S(2)}) collective-permute-start(f32[48,768]{1,0:T(8,128)S(1)} %copy-done.9), channel_id=1, source_target_pairs={{0,2},{2,0},{4,6},{6,4},{8,10},{10,8},{12,14},{14,12},{1,3},{3,1},... | collective-permute-start | bytes 442376 | tf_op jit(solution)/shard_map/ppermute | solution.py:471
  55.7 5.6 %collective-permute-start.9 = (f32[48,768]{1,0:T(8,128)S(1)}, f32[48,768]{1,0:T(8,128)S(1)}, u32[]{:S(2)}, u32[]{:S(2)}) collective-permute-start(f32[48,768]{1,0:T(8,128)S(1)} %add.49), channel_id=1, source_target_pairs={{0,4},{2,6},{4,0},{6,2},{8,12},{10,14},{12,8},{14,10},{1,5},{3,7},... | collective-permute-start | bytes 442376 | tf_op jit(solution)/shard_map/ppermute | solution.py:471
  61.3 8.8 %collective-permute-start.10 = (f32[48,768]{1,0:T(8,128)S(1)}, f32[48,768]{1,0:T(8,128)S(1)}, u32[]{:S(2)}, u32[]{:S(2)}) collective-permute-start(f32[48,768]{1,0:T(8,128)S(1)} %add.50), channel_id=1, source_target_pairs={{0,8},{2,10},{4,12},{6,14},{8,0},{10,2},{12,4},{14,6},{1,9},{3,11}... | collective-permute-start | bytes 442376 | tf_op jit(solution)/shard_map/ppermute | solution.py:471
  64.0 6.1 %collective-permute-start.7 = (f32[48,768]{1,0:T(8,128)S(1)}, f32[48,768]{1,0:T(8,128)S(1)}, u32[]{:S(2)}, u32[]{:S(2)}) collective-permute-start(f32[48,768]{1,0:T(8,128)S(1)} %copy-done.6), channel_id=1, source_target_pairs={{0,1},{1,0},{2,3},{3,2},{4,5},{5,4},{6,7},{7,6},{8,9},{9,8},{10,11... | collective-permute-start | bytes 442376 | tf_op jit(solution)/shard_map/ppermute | solution.py:464
  70.1 1.4 collective-permute-start.11
  95.1 17.8 %collective-permute-start.20 = (f32[12,64,768]{2,1,0:T(8,128)}, f32[12,64,768]{2,1,0:T(8,128)S(1)}, u32[]{:S(2)}, u32[]{:S(2)}) collective-permute-start(f32[12,64,768]{2,1,0:T(8,128)} %get-tuple-element.61.y_ref), channel_id=1, source_target_pairs={{0,1},{1,0},{2,3},{3,2},{4,5},{5,4},{6,7},{7,6},{8,9},{9,8},{10,11... | collective-permute-start | bytes 7077896 | tf_op jit(solution)/shard_map/ppermute | solution.py:464
  95.2 4.6 %collective-permute-start.12 = (f32[8,128]{1,0:T(8,128)}, f32[8,128]{1,0:T(8,128)S(1)}, u32[]{:S(2)}, u32[]{:S(2)}) collective-permute-start(f32[8,128]{1,0:T(8,128)} %get-tuple-element.54), channel_id=1, source_target_pairs={{0,1},{1,0},{2,3},{3,2},{4,5},{5,4},{6,7},{7,6},{8,9},{9,8},{10,11... | collective-permute-start | bytes 12296 | tf_op jit(solution)/shard_map/ppermute | solution.py:464
  100.6 3.6 %collective-permute-start.13 = (f32[8,128]{1,0:T(8,128)S(1)}, f32[8,128]{1,0:T(8,128)S(1)}, u32[]{:S(2)}, u32[]{:S(2)}) collective-permute-start(f32[8,128]{1,0:T(8,128)S(1)} %add.53), channel_id=1, source_target_pairs={{0,2},{2,0},{4,6},{6,4},{8,10},{10,8},{12,14},{14,12},{1,3},{3,1},... | collective-permute-start | bytes 12296 | tf_op jit(solution)/shard_map/ppermute | solution.py:471
  104.2 3.6 %collective-permute-start.14 = (f32[8,128]{1,0:T(8,128)S(1)}, f32[8,128]{1,0:T(8,128)S(1)}, u32[]{:S(2)}, u32[]{:S(2)}) collective-permute-start(f32[8,128]{1,0:T(8,128)S(1)} %add.54), channel_id=1, source_target_pairs={{0,4},{2,6},{4,0},{6,2},{8,12},{10,14},{12,8},{14,10},{1,5},{3,7},... | collective-permute-start | bytes 12296 | tf_op jit(solution)/shard_map/ppermute | solution.py:471
  107.8 4.5 %collective-permute-start.15 = (f32[8,128]{1,0:T(8,128)S(1)}, f32[8,128]{1,0:T(8,128)S(1)}, u32[]{:S(2)}, u32[]{:S(2)}) collective-permute-start(f32[8,128]{1,0:T(8,128)S(1)} %add.55), channel_id=1, source_target_pairs={{0,8},{2,10},{4,12},{6,14},{8,0},{10,2},{12,4},{14,6},{1,9},{3,11}... | collective-permute-start | bytes 12296 | tf_op jit(solution)/shard_map/ppermute | solution.py:471
  135.7 22.4 %collective-permute-start.21 = (f32[12,64,768]{2,1,0:T(8,128)}, f32[12,64,768]{2,1,0:T(8,128)S(1)}, u32[]{:S(2)}, u32[]{:S(2)}) collective-permute-start(f32[12,64,768]{2,1,0:T(8,128)} %get-tuple-element.69.bar_ref), channel_id=1, source_target_pairs={{0,1},{1,0},{2,3},{3,2},{4,5},{5,4},{6,7},{7,6},{8,9},{9,8},{10,11... | collective-permute-start | bytes 7077896 | tf_op jit(solution)/shard_map/ppermute | solution.py:464
  135.7 5.2 %collective-permute-start.16 = (f32[32,768]{1,0:T(8,128)S(1)}, f32[32,768]{1,0:T(8,128)S(1)}, u32[]{:S(2)}, u32[]{:S(2)}) collective-permute-start(f32[32,768]{1,0:T(8,128)S(1)} %constant_dynamic-update-slice_fusion), channel_id=1, source_target_pairs={{0,2},{2,0},{4,6},{6,4},{8,10},{10,8},{12,14},{14,12},{1,3},{3,1},... | collective-permute-start | bytes 294920 | tf_op jit(solution)/shard_map/ppermute | solution.py:471
  141.0 4.7 %collective-permute-start.17 = (f32[32,768]{1,0:T(8,128)S(1)}, f32[32,768]{1,0:T(8,128)S(1)}, u32[]{:S(2)}, u32[]{:S(2)}) collective-permute-start(f32[32,768]{1,0:T(8,128)S(1)} %add.57), channel_id=1, source_target_pairs={{0,4},{2,6},{4,0},{6,2},{8,12},{10,14},{12,8},{14,10},{1,5},{3,7},... | collective-permute-start | bytes 294920 | tf_op jit(solution)/shard_map/ppermute | solution.py:471
  145.7 6.6 %collective-permute-start.18 = (f32[32,768]{1,0:T(8,128)S(1)}, f32[32,768]{1,0:T(8,128)S(1)}, u32[]{:S(2)}, u32[]{:S(2)}) collective-permute-start(f32[32,768]{1,0:T(8,128)S(1)} %add.58), channel_id=1, source_target_pairs={{0,8},{2,10},{4,12},{6,14},{8,0},{10,2},{12,4},{14,6},{1,9},{3,11}... | collective-permute-start | bytes 294920 | tf_op jit(solution)/shard_map/ppermute | solution.py:471
  152.4 1.4 collective-permute-start.19
  (13 other events, 30.4 us)
